TPU v7x, 512 devices: a whole 4x4x16 slice. The times are simulated.
512 devices in a mesh: segment: 2 (over core), dp: 4 (over y), ep: 64 (over z, x).
Axes of the slice: x: 4, y: 4, z: 16, core: 2. Of those that a mesh axis runs over, the one named last changes fastest.
Arguments:
- cache_values: bfloat16 [2, 4, 2, 8192, 512], P('segment', 'dp', None, 'ep'), may hold values from -8 to 8
- cache_rope: bfloat16 [2, 4, 2, 64, 8192], P('segment', 'dp', None, None, 'ep'), may hold values from -6 to 6
- cache_scales: bfloat16 [2, 4, 2, 4, 8192], P('segment', 'dp', None, None, 'ep'), may hold values from 0.29882812 to 3
- queries: bfloat16 [2, 4, 2, 576, 256], P('segment', 'dp'), may hold values from -40 to 40
- new_keys: bfloat16 [2, 4, 2, 2, 576], P('segment', 'dp'), may hold values from -16 to 16
- hidden_rows: bfloat16 [2, 4, 2, 2, 3584], P('segment', 'dp'), may hold values from -6 to 6
- expert_ids: int32 [2, 4, 2, 2, 8], P('segment', 'dp'), may hold values from 0 to 127, all different within a row
- expert_gates: bfloat16 [2, 4, 2, 2, 8], P('segment', 'dp'), may hold values from 0.099609375 to 1
- owners: int32 [2, 4, 2], P('segment', 'dp'), may hold values from 0 to 3, as said below
- lengths: int32 [2, 4, 2], P('segment', 'dp'), may hold values from 1 to 8192, as said below
- up_weight: bfloat16 [128, 3584, 1024], P('ep', None, ('segment', 'dp')), may hold values from -0.09375 to 0.09375
- down_weight: bfloat16 [128, 1024, 3584], P('ep', ('segment', 'dp')), may hold values from -0.1875 to 0.1875
Outputs:
- attention: bfloat16 [2, 4, 4, 2, 128, 512], P('segment', 'dp', None, None, 'ep')
- expert_mix: bfloat16 [2, 4, 4, 2, 3584], P('segment', 'dp')
Inputs may be any that keep to these rules, and one draw needn't show every extreme that they name: The requests of one prefill group have different owners; in each section some owner receives a request from every prefill group. `lengths`: in each section some request has the full 8192 positions.
All inputs are finite; a program needn't handle non-finite values.
Results may differ from a plain program's by a relative error of at most 0.0075.
Values may be sent and summed in bfloat16 or wider, within the bound.
A program may use at most 64 MiB of HBM per device.

v0:
```python
import jax
import jax.numpy as jnp
from jax import lax
from jax.sharding import PartitionSpec as P

score_scale = 192.0 ** (-0.5)
block_width = 128
far_below = -1e30


def swapped(block, axis, distance):
    count = lax.axis_size(axis)
    route = []
    for low in range(count):
        high = low | 1 << distance
        if high != low and high < count:
            route += [(low, high), (high, low)]
    return lax.ppermute(block, axis, route)


def as_sent(value):

    def short(part):
        return part.astype(jnp.bfloat16) if part.dtype == jnp.float32 else part

    return jax.tree.map(short, value)


def bucket(source_array, picked, living):
    taken = jnp.take(source_array, picked, axis=0)
    shape = (living.shape[0],) + (1,) * (source_array.ndim - 1)
    return jnp.where(living.reshape(shape), taken, jnp.zeros_like(taken))


def block_terms(block_scores, valid_keys, key_values):
    masked = jnp.where(valid_keys, block_scores, far_below)
    peak_score = jnp.max(masked, axis=1)
    weights = jnp.where(valid_keys, jnp.exp(masked - peak_score[:, None, :]), 0.0)
    weight_sum = jnp.sum(weights, axis=1)
    block_out = jnp.einsum(
        "scq,sck->sqk", weights.astype(jnp.bfloat16), key_values, preferred_element_type=jnp.float32
    )
    return (peak_score, weight_sum, block_out)


def join_terms(first, second):
    top_score = jnp.maximum(first[0], second[0])
    early_factor = jnp.exp(first[0] - top_score)
    late_factor = jnp.exp(second[0] - top_score)
    return (
        top_score,
        first[1] * early_factor + second[1] * late_factor,
        first[2] * early_factor[..., None] + second[2] * late_factor[..., None],
    )


def shards(
    cache_values,
    cache_rope,
    cache_scales,
    queries,
    new_keys,
    hidden_rows,
    expert_ids,
    expert_gates,
    owners,
    lengths,
    up_weight,
    down_weight,
):
    crossed = swapped(
        (
            cache_values[0, 0],
            cache_rope[0, 0],
            cache_scales[0, 0],
            queries[0, 0],
            new_keys[0, 0],
            hidden_rows[0, 0],
            expert_ids[0, 0],
            expert_gates[0, 0],
            owners[0, 0],
            lengths[0, 0],
        ),
        "segment",
        0,
    )
    (
        stored,
        rotary,
        block_scales,
        query_cols,
        fresh_keys,
        token_rows,
        chosen,
        gate_values,
        owner_list,
        length_list,
    ) = crossed
    slot_count = lax.axis_size("dp")
    request_count = owner_list.shape[0]
    matches = owner_list[None, :] == jnp.arange(slot_count, dtype=jnp.int32)[:, None]
    picked = jnp.sum(
        jnp.where(matches, jnp.arange(request_count, dtype=jnp.int32)[None, :], 0), axis=1
    )
    living = jnp.any(matches, axis=1)
    received = (
        lax.all_to_all(
            bucket(stored, picked, living), "dp", split_axis=0, concat_axis=0, tiled=True
        ),
        lax.all_to_all(
            bucket(rotary, picked, living), "dp", split_axis=0, concat_axis=0, tiled=True
        ),
        lax.all_to_all(
            bucket(block_scales, picked, living), "dp", split_axis=0, concat_axis=0, tiled=True
        ),
        lax.all_to_all(
            bucket(query_cols, picked, living), "dp", split_axis=0, concat_axis=0, tiled=True
        ),
        lax.all_to_all(
            bucket(fresh_keys, picked, living), "dp", split_axis=0, concat_axis=0, tiled=True
        ),
        lax.all_to_all(
            bucket(token_rows, picked, living), "dp", split_axis=0, concat_axis=0, tiled=True
        ),
        lax.all_to_all(
            as_sent(bucket(chosen, picked, living)), "dp", split_axis=0, concat_axis=0, tiled=True
        ),
        lax.all_to_all(
            bucket(gate_values, picked, living), "dp", split_axis=0, concat_axis=0, tiled=True
        ),
        lax.all_to_all(
            as_sent(bucket(length_list, picked, living)),
            "dp",
            split_axis=0,
            concat_axis=0,
            tiled=True,
        ),
    )
    (
        stored,
        rotary,
        block_scales,
        query_cols,
        fresh_keys,
        token_rows,
        chosen,
        gate_values,
        length_list,
    ) = received
    positions = stored.shape[1]
    lat_width = stored.shape[2]
    blocked = stored.reshape((slot_count, positions, block_scales.shape[1], block_width)).astype(
        jnp.float32
    )
    factor = jnp.swapaxes(block_scales, 1, 2).astype(jnp.float32)[..., None]
    latent = (blocked * factor).reshape(stored.shape).astype(jnp.bfloat16)
    block_scores = (
        jnp.einsum(
            "sck,skq->scq", latent, query_cols[:, :lat_width], preferred_element_type=jnp.float32
        )
        + jnp.einsum(
            "src,srq->scq", rotary, query_cols[:, lat_width:], preferred_element_type=jnp.float32
        )
    ) * score_scale
    ep_index = lax.axis_index("ep")
    position = ep_index * positions + jnp.arange(positions, dtype=jnp.int32)
    valid_keys = position[None, :, None] < length_list[:, None, None]
    state = block_terms(block_scores, valid_keys, latent)
    column_count = query_cols.shape[2]
    new_count = fresh_keys.shape[1]
    head_count = column_count // new_count
    fresh_scores = (
        jnp.einsum("sjk,skq->sjq", fresh_keys, query_cols, preferred_element_type=jnp.float32)
        * score_scale
    )
    column_pos = jnp.arange(column_count, dtype=jnp.int32) // head_count
    fresh_pos = jnp.arange(new_count, dtype=jnp.int32)
    fresh_valid = ((fresh_pos[:, None] <= column_pos[None, :]) & (ep_index == 0))[None, :, :]
    state = join_terms(state, block_terms(fresh_scores, fresh_valid, fresh_keys[:, :, :lat_width]))
    top_score = lax.pmax(state[0], "ep")
    rescale = jnp.exp(state[0] - top_score)
    scaled_sum = (state[1] * rescale).reshape((slot_count, new_count, head_count))
    scaled_out = (state[2] * rescale[..., None]).reshape(
        (slot_count, new_count, head_count, lat_width)
    )
    sum_share, out_share = (
        lax.psum_scatter(scaled_sum, "ep", scatter_dimension=2, tiled=True),
        lax.psum_scatter(scaled_out, "ep", scatter_dimension=2, tiled=True),
    )
    attended = out_share / sum_share[..., None]
    alive = length_list > 0
    attention = jnp.where(alive[:, None, None, None], attended, 0.0).astype(jnp.bfloat16)[
        None, None
    ]
    model_width = token_rows.shape[2]
    own_rows = slot_count * new_count
    every_rows, every_chosen, every_gates = (
        lax.all_gather(
            token_rows.reshape((own_rows, model_width)), ("segment", "dp"), axis=0, tiled=True
        ),
        lax.all_gather(
            as_sent(chosen.reshape((own_rows, chosen.shape[2]))),
            ("segment", "dp"),
            axis=0,
            tiled=True,
        ),
        lax.all_gather(
            gate_values.reshape((own_rows, gate_values.shape[2])),
            ("segment", "dp"),
            axis=0,
            tiled=True,
        ),
    )
    local_experts = up_weight.shape[0]
    part_gates = every_gates.astype(jnp.float32)
    running = jnp.zeros((own_rows * lax.axis_size(("segment", "dp")), model_width), jnp.float32)
    for local_slot in range(local_experts):
        expert = ep_index * local_experts + local_slot
        weight = jnp.sum(jnp.where(every_chosen == expert, part_gates, 0.0), axis=1)
        hidden = jax.nn.silu(
            jnp.dot(every_rows, up_weight[local_slot], preferred_element_type=jnp.float32)
        ).astype(jnp.bfloat16)
        running = running + weight[:, None] * jnp.dot(
            hidden, down_weight[local_slot], preferred_element_type=jnp.float32
        )
    hidden_summed = lax.psum_scatter(running, ("segment", "dp"), scatter_dimension=0, tiled=True)
    group_rows = lax.psum(hidden_summed, "ep")
    expert_mix = group_rows.reshape((slot_count, new_count, model_width)).astype(jnp.bfloat16)[
        None, None
    ]
    return (attention, expert_mix)


def solution(mesh):
    placed = (
        P("segment", "dp", None, "ep", None),
        P("segment", "dp", None, None, "ep"),
        P("segment", "dp", None, None, "ep"),
        P("segment", "dp", None, None, None),
        P("segment", "dp", None, None, None),
        P("segment", "dp", None, None, None),
        P("segment", "dp", None, None, None),
        P("segment", "dp", None, None, None),
        P("segment", "dp", None),
        P("segment", "dp", None),
        P("ep", None, ("segment", "dp")),
        P("ep", ("segment", "dp"), None),
    )
    return jax.shard_map(
        shards,
        mesh=mesh,
        in_specs=placed,
        out_specs=(
            P("segment", "dp", None, None, "ep", None),
            P("segment", "dp", None, None, None),
        ),
        check_vma=False,
    )
```

profile of v0, /device:TPU:8, one launch (start us, length us, event | category | flops | bytes accessed | tf_op | source)
XLA Modules:
  0.0 621.6 jit_solution(7048662612482836398)
XLA Ops:
  8.0 1.9 collective-permute-start
  9.9 2.4 collective-permute-start.6
  12.3 1.9 collective-permute-start.4
  14.3 2.4 collective-permute-start.3
  16.7 1.9 collective-permute-start.2
  18.7 2.4 collective-permute-start.1
  21.3 0.7 collective-permute-done.1
  22.0 2.2 collective-permute-start.8
  24.2 0.6 gather_fusion
  25.0 11.9 %all_to_all.49 = s32[4,1,1]{2,1,0:T(1,128)S(1)} all-to-all(s32[4,1,1]{2,1,0:T(1,128)S(1)} %copy.30), channel_id=1, replica_groups=mesh['segment'=2,'dp'=4,'ep'=64] {'dp'}, dimensions={0} | all-to-all | bytes 32 | tf_op jit(solution)/shard_map/all_to_all | solution.py:131
  36.9 0.2 reduce
  37.2 1.9 collective-permute-start.7
  39.1 0.6 gather_fusion.7
  39.7 0.7 broadcast_select_fusion.5
  40.3 4.6 all-to-all-start.7
  45.0 2.1 collective-permute-start.5
  47.1 0.6 gather_fusion.6
  47.7 0.7 select_select_fusion.3
  48.3 0.4 all-to-all-done.7
  48.7 4.7 all-to-all-start.6
  53.4 18.0 %all_gather.10 = bf16[64,8]{1,0:T(8,128)(2,1)S(1)} all-gather(bf16[8,8]{1,0:T(8,128)(2,1)S(1)} %bitcast.57), channel_id=1, replica_groups=mesh['segment'=2,'dp'=4,'ep'=64] {'segment','dp'}, dimensions={0}, use_global_device_ids=true | all-gather | bytes 1152 | tf_op jit(solution)/shard_map/all_gather | solution.py:207
  71.3 21.3 %all_gather.9 = s32[64,8]{1,0:T(8,128)S(1)} all-gather(s32[8,8]{1,0:T(8,128)S(1)} %bitcast.56), channel_id=1, replica_groups=mesh['segment'=2,'dp'=4,'ep'=64] {'segment','dp'}, dimensions={0}, use_global_device_ids=true | all-gather | bytes 2304 | tf_op jit(solution)/shard_map/all_gather | solution.py:201
  92.8 1.9 collective-permute-start.9
  94.7 0.6 gather_fusion.2
  95.3 0.7 select_select_fusion.4
  95.9 5.1 all-to-all-start.2
  101.0 0.6 gather_fusion.5
  101.6 0.7 broadcast_select_fusion.3
  102.3 0.7 gather_fusion.8
  103.0 0.8 broadcast_select_fusion.1
  103.7 0.6 gather_fusion.1
  104.3 0.5 all-to-all-done.2
  104.9 4.7 all-to-all-start.8
  109.6 0.9 select_select_fusion.1
  110.5 3.2 all-to-all-done.8
  113.7 4.9 all-to-all-start.1
  118.8 0.6 mul.87
  119.4 0.4 mul.88
  119.8 0.6 gather_fusion.4
  120.4 0.6 gather_fusion.3
  121.0 1.2 select_select_fusion
  122.2 3.0 all-to-all-done.1
  125.2 5.0 all-to-all-start.3
  130.2 0.7 select_select_fusion.2
  130.9 28.5 %all_gather.11 = bf16[64,3584]{1,0:T(8,128)(2,1)S(1)} all-gather(bf16[8,3584]{1,0:T(8,128)(2,1)S(1)} %reshape.204), channel_id=1, replica_groups=mesh['segment'=2,'dp'=4,'ep'=64] {'segment','dp'}, dimensions={0}, use_global_device_ids=true | all-gather | bytes 516096 | tf_op jit(solution)/shard_map/all_gather | solution.py:198
  159.4 3.0 convolution_multiply_fusion.1
  162.4 3.2 fusion
  165.6 4.7 all-to-all-start.5
  170.3 1.1 fusion.4
  171.5 2.7 all-to-all-done.5
  174.2 4.7 all-to-all-start.4
  178.9 0.3 fusion.45
  179.2 3.9 all-to-all-done.4
  183.1 1.3 fusion.46
  184.4 146.3 %pmax.7 = f32[4,256]{1,0:T(4,128)S(1)} all-reduce(f32[4,256]{1,0:T(4,128)S(1)} %max.12), channel_id=1, replica_groups=mesh['segment'=2,'dp'=4,'ep'=64] {'ep'}, use_global_device_ids=true, to_apply=%region_4.5 | all-reduce | flops 1024 | bytes 8192 | tf_op jit(solution)/shard_map/pmax | solution.py:180
  330.8 0.2 fusion.16
  330.9 0.6 fusion.18
  331.6 0.7 add_multiply_fusion
  332.2 2.6 copy.33
  334.9 1.3 dynamic-slice
  337.0 275.1 %all-reduce.2 = (f32[4,2,128]{0,1,2:T(2,128)S(1)}, bf16[8,3584]{1,0:T(8,128)(2,1)S(1)}) all-reduce(f32[4,2,128]{0,1,2:T(2,128)S(1)} %copy.34, f32[8,3584]{1,0:T(8,128)} %reduce-scatter.2.cloned.1.call-done), channel_id=3, replica_groups=mesh['segment'=2,'dp'=4,'ep'=64] {'ep'}, use_global_device_ids=true, to_apply=%region_8.9.clone | all-reduce | flops 29696 | bytes 180224
  612.1 0.6 convert_element_type.55
  612.7 0.8 fusion.36
  613.6 0.6 copy.35
  (38 shorter events, 1.0 us)
Async XLA Ops:
  8.0 10.7 %collective-permute-start = (s32[2]{0:T(128)}, s32[2]{0:T(128)S(1)}, u32[]{:S(2)}, u32[]{:S(2)}) collective-permute-start(s32[2]{0:T(128)} %bitcast.66), channel_id=1, source_target_pairs={{0,256},{256,0},{1,257},{257,1},{2,258},{258,2},{3,259},{259,3},{4... | collective-permute-start | bytes 32 | tf_op jit(solution)/shard_map/ppermute | solution.py:18
  9.9 91.1 %collective-permute-start.6 = (bf16[2,2,576]{2,1,0:T(2,128)(2,1)}, bf16[2,2,576]{2,1,0:T(2,128)(2,1)S(1)}, u32[]{:S(2)}, u32[]{:S(2)}) collective-permute-start(bf16[2,2,576]{2,1,0:T(2,128)(2,1)} %bitcast.62), channel_id=1, source_target_pairs={{0,256},{256,0},{1,257},{257,1},{2,258},{258,2},{3,259},{259,3},{4... | collective-permute-start | bytes 13832 | tf_op jit(solution)/shard_map/ppermute | solution.py:18
  12.3 108.1 %collective-permute-start.4 = (bf16[2,576,256]{2,1,0:T(8,128)(2,1)}, bf16[2,576,256]{2,1,0:T(8,128)(2,1)S(1)}, u32[]{:S(2)}, u32[]{:S(2)}) collective-permute-start(bf16[2,576,256]{2,1,0:T(8,128)(2,1)} %bitcast.58), channel_id=1, source_target_pairs={{0,256},{256,0},{1,257},{257,1},{2,258},{258,2},{3,259},{259,3},{4... | collective-permute-start | bytes 1769480 | tf_op jit(solution)/shard_map/ppermute | solution.py:18
  14.3 78.5 %collective-permute-start.3 = (bf16[2,4,128]{2,1,0:T(4,128)(2,1)}, bf16[2,4,128]{2,1,0:T(4,128)(2,1)S(1)}, u32[]{:S(2)}, u32[]{:S(2)}) collective-permute-start(bf16[2,4,128]{2,1,0:T(4,128)(2,1)} %bitcast.64), channel_id=1, source_target_pairs={{0,256},{256,0},{1,257},{257,1},{2,258},{258,2},{3,259},{259,3},{4... | collective-permute-start | bytes 6152 | tf_op jit(solution)/shard_map/ppermute | solution.py:18
  16.7 87.1 %collective-permute-start.2 = (bf16[2,128,512]{2,1,0:T(8,128)(2,1)}, bf16[2,128,512]{2,1,0:T(8,128)(2,1)S(1)}, u32[]{:S(2)}, u32[]{:S(2)}) collective-permute-start(bf16[2,128,512]{2,1,0:T(8,128)(2,1)} %bitcast.59), channel_id=1, source_target_pairs={{0,256},{256,0},{1,257},{257,1},{2,258},{258,2},{3,259},{259,3},{4... | collective-permute-start | bytes 786440 | tf_op jit(solution)/shard_map/ppermute | solution.py:18
  18.7 3.3 collective-permute-start.1
  22.0 15.1 %collective-permute-start.8 = (bf16[2,2,8]{2,1,0:T(2,128)(2,1)}, bf16[2,2,8]{2,1,0:T(2,128)(2,1)S(1)}, u32[]{:S(2)}, u32[]{:S(2)}) collective-permute-start(bf16[2,2,8]{2,1,0:T(2,128)(2,1)} %bitcast.65), channel_id=1, source_target_pairs={{0,256},{256,0},{1,257},{257,1},{2,258},{258,2},{3,259},{259,3},{4... | collective-permute-start | bytes 200 | tf_op jit(solution)/shard_map/ppermute | solution.py:18
  37.2 7.8 %collective-permute-start.7 = (s32[2,2,8]{2,1,0:T(2,128)}, s32[2,2,8]{2,1,0:T(2,128)S(1)}, u32[]{:S(2)}, u32[]{:S(2)}) collective-permute-start(s32[2,2,8]{2,1,0:T(2,128)} %bitcast.63), channel_id=1, source_target_pairs={{0,256},{256,0},{1,257},{257,1},{2,258},{258,2},{3,259},{259,3},{4... | collective-permute-start | bytes 392 | tf_op jit(solution)/shard_map/ppermute | solution.py:18
  40.3 8.4 %all-to-all-start.7 = ((bf16[4,2,8]{2,1,0:T(2,128)(2,1)}), bf16[4,2,8]{2,1,0:T(2,128)(2,1)S(1)}, u32[]{:S(2)}, u32[]{:S(2)}) async-start(bf16[4,2,8]{2,1,0:T(2,128)(2,1)} %broadcast_select_fusion.5), calls=%async_computation.7 | async-start | bytes 4096 | tf_op jit(solution)/shard_map/all_to_all | solution.py:128
  45.0 74.8 %collective-permute-start.5 = (bf16[2,64,128]{2,1,0:T(8,128)(2,1)}, bf16[2,64,128]{2,1,0:T(8,128)(2,1)S(1)}, u32[]{:S(2)}, u32[]{:S(2)}) collective-permute-start(bf16[2,64,128]{2,1,0:T(8,128)(2,1)} %bitcast.60), channel_id=1, source_target_pairs={{0,256},{256,0},{1,257},{257,1},{2,258},{258,2},{3,259},{259,3},{4... | collective-permute-start | bytes 98312 | tf_op jit(solution)/shard_map/ppermute | solution.py:18
  48.7 22.6 %all-to-all-start.6 = ((s32[4,2,8]{2,1,0:T(2,128)}), s32[4,2,8]{2,1,0:T(2,128)S(1)}, u32[]{:S(2)}, u32[]{:S(2)}) async-start(s32[4,2,8]{2,1,0:T(2,128)} %select_select_fusion.3), calls=%async_computation.6 | async-start | bytes 8192 | tf_op jit(solution)/shard_map/all_to_all | solution.py:125
  92.8 9.6 %collective-permute-start.9 = (bf16[2,2,3584]{2,1,0:T(2,128)(2,1)}, bf16[2,2,3584]{2,1,0:T(2,128)(2,1)S(1)}, u32[]{:S(2)}, u32[]{:S(2)}) collective-permute-start(bf16[2,2,3584]{2,1,0:T(2,128)(2,1)} %bitcast.61), channel_id=1, source_target_pairs={{0,256},{256,0},{1,257},{257,1},{2,258},{258,2},{3,259},{259,3},{4... | collective-permute-start | bytes 86024 | tf_op jit(solution)/shard_map/ppermute | solution.py:18
  95.9 8.9 %all-to-all-start.2 = ((bf16[4,4,128]{2,1,0:T(4,128)(2,1)}), bf16[4,4,128]{2,1,0:T(4,128)(2,1)S(1)}, u32[]{:S(2)}, u32[]{:S(2)}) async-start(bf16[4,4,128]{2,1,0:T(4,128)(2,1)} %select_select_fusion.4), calls=%async_computation.2 | async-start | bytes 8192 | tf_op jit(solution)/shard_map/all_to_all | solution.py:113
  104.9 8.8 %all-to-all-start.8 = ((bf16[4,2,3584]{2,1,0:T(2,128)(2,1)}), bf16[4,2,3584]{2,1,0:T(2,128)(2,1)S(1)}, u32[]{:S(2)}, u32[]{:S(2)}) async-start(bf16[4,2,3584]{2,1,0:T(2,128)(2,1)} %broadcast_select_fusion.1), calls=%async_computation.8 | async-start | bytes 114688 | tf_op jit(solution)/shard_map/all_to_all | solution.py:122
  113.7 11.5 %all-to-all-start.1 = ((bf16[4,128,512]{2,1,0:T(8,128)(2,1)}), bf16[4,128,512]{2,1,0:T(8,128)(2,1)S(1)}, u32[]{:S(2)}, u32[]{:S(2)}) async-start(bf16[4,128,512]{2,1,0:T(8,128)(2,1)} %select_select_fusion.1), calls=%async_computation.1 | async-start | bytes 1048576 | tf_op jit(solution)/shard_map/all_to_all | solution.py:107
  125.2 40.4 %all-to-all-start.3 = ((bf16[4,576,256]{2,1,0:T(8,128)(2,1)}), bf16[4,576,256]{2,1,0:T(8,128)(2,1)S(1)}, u32[]{:S(2)}, u32[]{:S(2)}) async-start(bf16[4,576,256]{2,1,0:T(8,128)(2,1)} %select_select_fusion), calls=%async_computation.3 | async-start | bytes 2359296 | tf_op jit(solution)/shard_map/all_to_all | solution.py:116
  130.2 206.8 %reduce-scatter.2.cloned.1.call-start = ((), (), s32[]{:S(2)}) async-start(), calls=%async_computation.10 | async-start | bytes 1032192 | tf_op jit(solution)/shard_map/reduce_scatter | solution.py:226
  165.6 8.6 %all-to-all-start.5 = ((bf16[4,2,576]{2,1,0:T(2,128)(2,1)}), bf16[4,2,576]{2,1,0:T(2,128)(2,1)S(1)}, u32[]{:S(2)}, u32[]{:S(2)}) async-start(bf16[4,2,576]{2,1,0:T(2,128)(2,1)} %broadcast_select_fusion.3), calls=%async_computation.5 | async-start | bytes 20480 | tf_op jit(solution)/shard_map/all_to_all | solution.py:119
  174.2 8.9 %all-to-all-start.4 = ((bf16[4,64,128]{2,1,0:T(8,128)(2,1)}), bf16[4,64,128]{2,1,0:T(8,128)(2,1)S(1)}, u32[]{:S(2)}, u32[]{:S(2)}) async-start(bf16[4,64,128]{2,1,0:T(8,128)(2,1)} %select_select_fusion.2), calls=%async_computation.4 | async-start | bytes 131072 | tf_op jit(solution)/shard_map/all_to_all | solution.py:110
  178.9 433.8 %all-reduce.5.cloned.1.call-start = ((), (), s32[]{:S(2)}) async-start(), calls=%async_computation.11 | async-start | bytes 4194304
Sparse Core Ops, SparseCore 0:
  165.7 40.3 reduce-scatter.1
Sparse Core Ops, SparseCore 1:
  335.0 270.0 all-reduce.4
where the time goes:
time: 623 us; the launch traced here: 622 us
  blocking collectives  501 us (80%)
  starting transfers between devices  59.5 us (10%)
  between operations  16.4 us (3%)
  waiting for transfers between devices  14.5 us (2%)
  local copies, waits for them, and re-layouts  12 us (2%)
  matrix products  10.2 us (2%)
  other arithmetic  7.9 us (1%)
    unnamed x1, blocking collectives  275 us
    pmax x1, blocking collectives, shards(): top_score = lax.pmax(state[0], 'ep')  146 us
    all_gather x1, blocking collectives, shards(): lax.all_gather(token_rows.reshape((own_rows, model_width)), ('segment', '...  28.5 us
    all_gather x1, blocking collectives, shards(): lax.all_gather(as_sent(chosen.reshape((own_rows, chosen.shape[2]))), ('se...  21.3 us
    ppermute x10, starting transfers between devices, swapped(): return lax.ppermute(block, axis, route)  21.1 us
    all_gather x1, blocking collectives, shards(): lax.all_gather(gate_values.reshape((own_rows, gate_values.shape[2])), ('s...  18 us
  transfers between devices with their start and end apart: 20, of which 7 were waited for; matrix products, arithmetic and copies ran while one was open for 5% of the time, Pallas kernels for 0%

commit v1 on v0

v1 whole, which is shorter than its diff:
```python
import functools

import jax
import jax.numpy as jnp
from jax import lax
from jax.experimental import pallas as pl
from jax.experimental.pallas import tpu as pltpu
from jax.sharding import PartitionSpec as P

score_scale = 192.0 ** (-0.5)
far_below = -1e30
x_chips = 4
MESH = pl.DeviceIdType.MESH
f32 = jnp.float32
bf16 = jnp.bfloat16


def iota(shape, dim):
    return lax.broadcasted_iota(jnp.int32, shape, dim)


def dot(a, b):
    return jnp.dot(a, b, preferred_element_type=f32)


def dot_rows(a, b):
    return lax.dot_general(a, b, (((1,), (1,)), ((), ())), preferred_element_type=f32)


def dot_cols(a, b):
    return lax.dot_general(a, b, (((0,), (0,)), ((), ())), preferred_element_type=f32)


def three_parts(value):
    high = value.astype(bf16).astype(f32)
    rest = value - high
    middle = rest.astype(bf16).astype(f32)
    low = (rest - middle).astype(bf16).astype(f32)
    return high, middle, low


def kernel(
    sizes,
    cv_h, q_h, up_h, dn_h, cr, cs, nk, xr, ids, gates, owners, lengths,
    attn_o, mix_o,
    cv, q, up, dn, tr, nkp, xf, xg,
    a1s, a1r, t1s, t1r, a2s, a2r, a3s, a3r,
    e1s, e1r, e2s, e2r, e3s, e3r, e4, e4f, e5x, e5y,
    in_sem,
    e0_ss, e0_rs, a1_ss, a1_rs, t1_ss, t1_rs, a2_ss, a2_rs, a3_ss, a3_rs,
    e1_ss, e1_rs, e2_ss, e2_rs, e3_ss, e3_rs, e4_ss, e4_rs, e5x_ss, e5x_rs, e5y_ss, e5y_rs,
):
    nd, ny, nz, nx = sizes
    s, y, ep = lax.axis_index("segment"), lax.axis_index("dp"), lax.axis_index("ep")
    z, x = ep // nx, lax.rem(ep, nx)
    d = s * ny + y
    ctx, lat = cv.shape[1], cv.shape[2]
    cols = q.shape[2]
    heads = cols // 2
    hl = heads // (nz * nx)
    width = up.shape[1]
    quarter = width // 4
    ycols = width // ny
    xcols = e2s.shape[2]
    rows_x = a1s.shape[1]
    sec = ny * 4

    loads = [
        pltpu.make_async_copy(a, b, in_sem.at[i])
        for i, (a, b) in enumerate(((cv_h, cv), (q_h, q), (up_h, up), (dn_h, dn)))
    ]
    for load in loads:
        load.start()

    def plane(k):
        to = lax.rem(d + k, nd)
        return to, {"segment": to // ny, "dp": lax.rem(to, ny)}

    def along_x(k):
        to = lax.rem(x + k, nx)
        return to, {"ep": z * nx + to}

    def along_z(k):
        to = lax.rem(z + k, nz)
        return to, {"ep": to * nx + x}

    def along_y(k):
        to = lax.rem(y + k, ny)
        return to, {"dp": to}

    def across(k):
        to = lax.rem(y + k, ny)
        return to, {"segment": 1 - s, "dp": to}

    def remote(src, dst, ss, rs, k, to):
        return pltpu.make_async_remote_copy(
            src_ref=src, dst_ref=dst, send_sem=ss.at[k], recv_sem=rs.at[k],
            device_id=to, device_id_type=MESH,
        )

    def c_e0(k):
        return remote(xg.at[d], xg.at[d], e0_ss, e0_rs, k, plane(k)[1])

    def c_a1(k):
        to, dev = along_x(k)
        return remote(a1s.at[to], a1r.at[k], a1_ss, a1_rs, k, dev)

    def c_t1(k):
        to, dev = along_x(k)
        return remote(t1s.at[to], t1r.at[k], t1_ss, t1_rs, k, dev)

    def c_a2(k):
        to, dev = along_z(k)
        return remote(a2s.at[to], a2r.at[k], a2_ss, a2_rs, k, dev)

    def c_a3(k):
        return remote(a3s, a3r.at[y], a3_ss, a3_rs, k, across(k)[1])

    def c_e1(k):
        to, dev = plane(k)
        return remote(e1s.at[to], e1r.at[k], e1_ss, e1_rs, k, dev)

    def c_e2(k):
        to, dev = along_x(k)
        return remote(e2s.at[to], e2r.at[k], e2_ss, e2_rs, k, dev)

    def c_e3(k):
        to, dev = along_z(k)
        return remote(e3s.at[to], e3r.at[k], e3_ss, e3_rs, k, dev)

    def c_e4(k):
        return remote(e4.at[z], e4.at[z], e4_ss, e4_rs, k, along_z(k)[1])

    def c_e5x(k):
        return remote(e5x.at[x], e5x.at[x], e5x_ss, e5x_rs, k, along_x(k)[1])

    def c_e5y(k):
        return remote(e5y.at[y], e5y.at[y], e5y_ss, e5y_rs, k, along_y(k)[1])

    def each(first, last, act):
        def body(k, carry):
            act(k)
            return carry

        lax.fori_loop(first, last, body, 0)

    barrier = pltpu.get_barrier_semaphore()

    def greet(where):
        def act(k):
            pl.semaphore_signal(barrier, inc=1, device_id=where(k)[1], device_id_type=MESH)

        return act

    each(1, nd, greet(plane))
    each(1, nx, greet(along_x))
    each(1, nz, greet(along_z))

    xf[...] = jnp.zeros_like(xf)
    for r in range(2):
        for j in range(2):
            i = 2 * r + j
            row = xr[r, j:j + 1, :].astype(f32)
            for part in range(4):
                xf[4 * i + part:4 * i + part + 1, :quarter] = row[:, part * quarter:(part + 1) * quarter]
            xf[4 * i:4 * i + 1, quarter:quarter + 8] = ids[r, j:j + 1, :].astype(f32)
            xf[4 * i + 1:4 * i + 2, quarter:quarter + 8] = gates[r, j:j + 1, :].astype(f32)
            xf[4 * i + 2:4 * i + 3, quarter:] = jnp.full((1, 128), owners[r], jnp.int32).astype(f32)
    xg[d] = xf[...].astype(bf16)

    pl.semaphore_wait(barrier, (nd - 1) + (nx - 1) + (nz - 1))
    each(1, nd, lambda k: c_e0(k).start())

    tr[...] = jnp.zeros_like(tr)
    nkp[...] = jnp.zeros_like(nkp)
    for r in range(2):
        tr[8 * r:8 * r + 4, :ctx] = cs[r].astype(f32)
        nkp[16 * r:16 * r + 2, :] = nk[r].astype(f32)
    scale_cols = tr[:, :ctx].T
    total_rows = nx * rows_x
    place = iota((total_rows, cols), 0)
    per = 2 * hl
    h_of = lax.rem(place, hl)
    j_of = lax.rem(place // hl, 2)
    r_of = lax.rem(place // per, 2)
    z_of = lax.rem(place // (2 * per), nz)
    x_of = place // (2 * per * nz)
    match = (j_of * heads + (z_of * nx + x_of) * hl + h_of) == iota((total_rows, cols), 1)
    loads[0].wait()
    loads[1].wait()
    out = jnp.zeros((total_rows, lat), f32)
    stats = jnp.zeros((16, total_rows), f32)
    for r in range(2):
        latent = jnp.concatenate(
            [
                cv[r, :, b * 128:(b + 1) * 128].astype(f32) * scale_cols[:, 8 * r + b:8 * r + b + 1]
                for b in range(lat // 128)
            ],
            axis=1,
        ).astype(bf16)
        fresh = nkp[16 * r:16 * r + 16, :].astype(bf16)
        cached = dot(latent, q[r, :lat, :]) + dot_cols(cr[r], q[r, lat:, :])
        newer = dot(fresh[:, :lat], q[r, :lat, :]) + dot(fresh[:, lat:], q[r, lat:, :])
        cached_ok = ep * ctx + iota((ctx, cols), 0) < lengths[r]
        newer_ok = (iota((16, cols), 0) + jnp.where(ep == 0, 0, 16)) <= (iota((16, cols), 1) // heads)
        cached = jnp.where(cached_ok, cached * score_scale, far_below)
        newer = jnp.where(newer_ok, newer * score_scale, far_below)
        peak = jnp.maximum(
            jnp.max(cached, axis=0, keepdims=True), jnp.max(newer, axis=0, keepdims=True)
        )
        cached = jnp.where(cached_ok, jnp.exp(cached - peak), 0.0)
        newer = jnp.where(newer_ok, jnp.exp(newer - peak), 0.0)
        total = jnp.sum(cached, axis=0, keepdims=True) + jnp.sum(newer, axis=0, keepdims=True)
        line = iota((16, cols), 0)
        extra = jnp.zeros((16, cols), f32)
        for n, part in enumerate(three_parts(peak) + three_parts(total)):
            extra = jnp.where(line == n, part, extra)
        order = jnp.where(match & (r_of == r), 1.0, 0.0).astype(bf16)
        out = out + dot(dot_rows(order, cached.astype(bf16)).astype(bf16), latent)
        out = out + dot(dot_rows(order, newer.astype(bf16)).astype(bf16), fresh[:, :lat])
        stats = stats + dot_rows(extra.astype(bf16), order)
    peak = stats[0:1] + stats[1:2] + stats[2:3]
    total = stats[3:4] + stats[4:5] + stats[5:6]
    for to in range(nx):
        a1s[to] = out[to * rows_x:(to + 1) * rows_x].astype(bf16)
        t1s[to, 0:1, :] = peak[:, to * rows_x:(to + 1) * rows_x]
        t1s[to, 1:2, :] = total[:, to * rows_x:(to + 1) * rows_x]
        t1s[to, 2:8, :] = jnp.zeros((6, rows_x), f32)
    each(1, nx, lambda k: c_t1(k).start())
    each(1, nx, lambda k: c_a1(k).start())

    each(1, nd, lambda k: c_e0(k).wait_recv())
    loads[2].wait()
    loads[3].wait()
    gathered = xg[...].reshape((nd * 16, xg.shape[2]))
    notes = gathered[:, quarter:]
    row_count = nd * 4
    want = iota((3 * row_count, nd * 16), 0)
    pick = iota((3 * row_count, nd * 16), 1) == 4 * lax.rem(want, row_count) + want // row_count
    pick = jnp.where(pick, 1.0, 0.0).astype(bf16)
    routing = dot(pick, notes)
    chosen, gate_values = routing[:row_count], routing[row_count:2 * row_count]
    lane = iota((row_count, 128), 1)
    part_of = lax.rem(iota((nd * 16, up.shape[2]), 0), 4)
    partial = jnp.zeros((row_count, width), f32)
    for e in range(up.shape[0]):
        expert = (ep * up.shape[0] + e).astype(f32)
        gate = jnp.sum(
            jnp.where((chosen == expert) & (lane < 8), gate_values, 0.0), axis=1, keepdims=True
        )
        acc = jnp.zeros((nd * 16, up.shape[2]), f32)
        for part in range(4):
            piece = dot(gathered[:, :quarter], up[e, part * quarter:(part + 1) * quarter, :])
            acc = jnp.where(part_of == part, piece, acc)
        acc = acc + pltpu.roll(acc, nd * 16 - 1, 0)
        acc = acc + pltpu.roll(acc, nd * 16 - 2, 0)
        hidden = (acc / (1.0 + jnp.exp(-acc))).astype(bf16)
        hidden = dot(pick[:row_count], hidden).astype(bf16)
        partial = partial + gate * dot(hidden, dn[e])
    for c in range(2):
        for to in range(ny):
            e1s[c * ny + to] = partial[
                (1 - c) * sec:(2 - c) * sec, to * ycols:(to + 1) * ycols
            ].astype(bf16)
    each(1, nd, lambda k: c_e1(k).start())

    first_row = jnp.where(s == 0, ny * 16, 0)
    owner_lane = jnp.where(iota((16, 128), 1) == 0, 1.0, 0.0).astype(bf16)

    def owner_row(count, split):
        row = iota((count, nd * 16), 0)
        spot = first_row + 4 * (row // split) + 2
        pull = jnp.where(iota((count, nd * 16), 1) == spot, 1.0, 0.0).astype(bf16)
        return dot_rows(owner_lane, dot(pull, notes).astype(bf16))[0:1]

    mine = y.astype(f32)
    out_i, in_i = iota((2 * ny, sec), 0), iota((2 * ny, sec), 1)
    mix_pick = (out_i // 2 == in_i // 4) & (lax.rem(out_i, 2) == lax.rem(in_i, 2))
    mix_pick = jnp.where(mix_pick & (owner_row(sec, 1) == mine), 1.0, 0.0).astype(bf16)
    out_i, in_i = iota((2 * per // 2 * ny, 2 * per * ny), 0), iota((2 * per // 2 * ny, 2 * per * ny), 1)
    attn_pick = (out_i // per == in_i // (2 * per)) & (lax.rem(out_i, per) == lax.rem(in_i, per))
    attn_pick = jnp.where(attn_pick & (owner_row(2 * per * ny, hl) == mine), 1.0, 0.0).astype(bf16)

    each(1, nx, lambda k: c_t1(k).wait_recv())
    tops = [t1s[x, 0:1, :]] + [t1r[k, 0:1, :] for k in range(1, nx)]
    sums = [t1s[x, 1:2, :]] + [t1r[k, 1:2, :] for k in range(1, nx)]
    top = functools.reduce(jnp.maximum, tops)
    factors = [jnp.exp(one - top) for one in tops]
    total = functools.reduce(jnp.add, [a * b for a, b in zip(factors, sums)])
    tr[...] = jnp.zeros_like(tr)
    for n, one in enumerate(list(three_parts(top) + three_parts(total)) + factors):
        tr[n:n + 1, :rows_x] = one
    turned = tr[:, :rows_x].T
    each(1, nx, lambda k: c_a1(k).wait_recv())
    merged = turned[:, 6:7] * a1s[x].astype(f32)
    for k in range(1, nx):
        merged = merged + turned[:, 6 + k:7 + k] * a1r[k].astype(f32)
    a2s[:, :, :lat] = merged.reshape((nz, 2 * per, lat)).astype(bf16)
    a2s[:, :, lat:] = turned.reshape((nz, 2 * per, 128)).astype(bf16)
    each(1, nz, lambda k: c_a2(k).start())

    each(1, nd, lambda k: c_e1(k).wait_recv())
    summed = e1s[d].astype(f32)
    for k in range(1, nd):
        summed = summed + e1r[k].astype(f32)
    for to in range(nx):
        low, high = to * xcols, min((to + 1) * xcols, ycols)
        e2s[to, :, :high - low] = summed[:, low:high].astype(bf16)
        if high - low < xcols:
            e2s[to, :, high - low:] = jnp.zeros((sec, xcols - (high - low)), bf16)
    each(1, nx, lambda k: c_e2(k).start())
    each(1, nx, lambda k: c_e2(k).wait_recv())
    summed = e2s[x].astype(f32)
    for k in range(1, nx):
        summed = summed + e2r[k].astype(f32)
    rz = sec // nz
    for to in range(nz):
        e3s[to] = summed[to * rz:(to + 1) * rz]
    each(1, nz, lambda k: c_e3(k).start())
    each(1, nz, lambda k: c_e3(k).wait_recv())
    summed = e3s[z]
    for k in range(1, nz):
        summed = summed + e3r[k]
    e4[z] = summed
    each(1, nz, lambda k: c_e4(k).start())

    a2r[0] = a2s[z]
    each(1, nz, lambda k: c_a2(k).wait_recv())
    arrived = a2r[...].astype(f32)
    tops = arrived[:, :, lat:lat + 1] + arrived[:, :, lat + 1:lat + 2] + arrived[:, :, lat + 2:lat + 3]
    sums = arrived[:, :, lat + 3:lat + 4] + arrived[:, :, lat + 4:lat + 5] + arrived[:, :, lat + 5:lat + 6]
    factors = jnp.exp(tops - jnp.max(tops, axis=0, keepdims=True))
    total = jnp.sum(factors * sums, axis=0)
    a3s[...] = (jnp.sum(factors * arrived[:, :, :lat], axis=0) / total).astype(bf16)
    each(0, ny, lambda k: c_a3(k).start())

    each(1, nz, lambda k: c_e4(k).wait_recv())
    for k in range(nz):
        e4f[k * rz:(k + 1) * rz, :] = e4[k]
    e5x[x] = e4f[...].astype(bf16)
    each(1, nx, lambda k: c_e5x(k).start())
    each(1, nx, lambda k: c_e5x(k).wait_recv())
    for k in range(nx):
        low, high = k * xcols, min((k + 1) * xcols, ycols)
        e5y[y, :, low:high] = e5x[k, :, :high - low]
    each(1, ny, lambda k: c_e5y(k).start())

    each(0, ny, lambda k: c_a3(k).wait_recv())
    finished = a3r[...].astype(f32).reshape((ny * 2 * per, lat)).astype(bf16)
    attn_o[...] = dot(attn_pick, finished).astype(bf16)

    each(1, ny, lambda k: c_e5y(k).wait_recv())
    for k in range(ny):
        mix_o[:, k * ycols:(k + 1) * ycols] = dot(mix_pick, e5y[k]).astype(bf16)

    def finish(k, carry):
        return carry

    each(1, nd, lambda k: c_e0(k).wait_send())
    each(1, nx, lambda k: c_t1(k).wait_send())
    each(1, nx, lambda k: c_a1(k).wait_send())
    each(1, nz, lambda k: c_a2(k).wait_send())
    each(0, ny, lambda k: c_a3(k).wait_send())
    each(1, nd, lambda k: c_e1(k).wait_send())
    each(1, nx, lambda k: c_e2(k).wait_send())
    each(1, nz, lambda k: c_e3(k).wait_send())
    each(1, nz, lambda k: c_e4(k).wait_send())
    each(1, nx, lambda k: c_e5x(k).wait_send())
    each(1, ny, lambda k: c_e5y(k).wait_send())


def shards(
    cache_values, cache_rope, cache_scales, queries, new_keys, hidden_rows,
    expert_ids, expert_gates, owners, lengths, up_weight, down_weight,
):
    ny = lax.axis_size("dp")
    nd = ny * lax.axis_size("segment")
    nx = x_chips
    nz = lax.axis_size("ep") // nx
    cv, cr, cs, q = cache_values[0, 0], cache_rope[0, 0], cache_scales[0, 0], queries[0, 0]
    nk, xr, ids, gates = new_keys[0, 0], hidden_rows[0, 0], expert_ids[0, 0], expert_gates[0, 0]
    ctx, lat = cv.shape[1:]
    cols = q.shape[2]
    heads = cols // 2
    hl = heads // (nz * nx)
    width = up_weight.shape[1]
    ycols = width // ny
    xcols = -(-ycols // (nx * 128)) * 128
    sec = ny * 4
    rows_x = nz * 4 * hl
    vmem = pl.BlockSpec(memory_space=pltpu.VMEM)
    smem = pl.BlockSpec(memory_space=pltpu.SMEM)
    anywhere = pl.BlockSpec(memory_space=pl.ANY)
    sems = lambda n: pltpu.SemaphoreType.DMA((n,))
    attention, mix = pl.pallas_call(
        functools.partial(kernel, (nd, ny, nz, nx)),
        out_shape=(
            jax.ShapeDtypeStruct((ny * 2 * hl, lat), bf16),
            jax.ShapeDtypeStruct((ny * 2, width), bf16),
        ),
        in_specs=[anywhere] * 4 + [vmem] * 6 + [smem] * 2,
        out_specs=(vmem, vmem),
        scratch_shapes=[
            pltpu.VMEM(cv.shape, bf16),
            pltpu.VMEM(q.shape, bf16),
            pltpu.VMEM(up_weight.shape, bf16),
            pltpu.VMEM(down_weight.shape, bf16),
            pltpu.VMEM((128, 128), f32),
            pltpu.VMEM((32, nk.shape[2]), f32),
            pltpu.VMEM((16, width // 4 + 128), f32),
            pltpu.VMEM((nd, 16, width // 4 + 128), bf16),
            pltpu.VMEM((nx, rows_x, lat), bf16),
            pltpu.VMEM((nx, rows_x, lat), bf16),
            pltpu.VMEM((nx, 8, rows_x), f32),
            pltpu.VMEM((nx, 8, rows_x), f32),
            pltpu.VMEM((nz, 4 * hl, lat + 128), bf16),
            pltpu.VMEM((nz, 4 * hl, lat + 128), bf16),
            pltpu.VMEM((4 * hl, lat), bf16),
            pltpu.VMEM((ny, 4 * hl, lat), bf16),
            pltpu.VMEM((nd, sec, ycols), bf16),
            pltpu.VMEM((nd, sec, ycols), bf16),
            pltpu.VMEM((nx, sec, xcols), bf16),
            pltpu.VMEM((nx, sec, xcols), bf16),
            pltpu.VMEM((nz, sec // nz, xcols), f32),
            pltpu.VMEM((nz, sec // nz, xcols), f32),
            pltpu.VMEM((nz, sec // nz, xcols), f32),
            pltpu.VMEM((sec, xcols), f32),
            pltpu.VMEM((nx, sec, xcols), bf16),
            pltpu.VMEM((ny, sec, ycols), bf16),
            sems(4),
            sems(nd), sems(nd), sems(nx), sems(nx), sems(nx), sems(nx), sems(nz), sems(nz),
            sems(ny), sems(ny),
            sems(nd), sems(nd), sems(nx), sems(nx), sems(nz), sems(nz), sems(nz), sems(nz),
            sems(nx), sems(nx), sems(ny), sems(ny),
        ],
        compiler_params=pltpu.CompilerParams(
            collective_id=0, has_side_effects=True, vmem_limit_bytes=60 * 1024 * 1024
        ),
    )(cv, q, up_weight, down_weight, cr, cs, nk, xr, ids, gates, owners[0, 0], lengths[0, 0])
    return (
        attention.reshape((1, 1, ny, 2, hl, lat)),
        mix.reshape((1, 1, ny, 2, width)),
    )


def solution(mesh):
    placed = (
        P("segment", "dp", None, "ep", None),
        P("segment", "dp", None, None, "ep"),
        P("segment", "dp", None, None, "ep"),
        P("segment", "dp", None, None, None),
        P("segment", "dp", None, None, None),
        P("segment", "dp", None, None, None),
        P("segment", "dp", None, None, None),
        P("segment", "dp", None, None, None),
        P("segment", "dp", None),
        P("segment", "dp", None),
        P("ep", None, ("segment", "dp")),
        P("ep", ("segment", "dp"), None),
    )
    return jax.shard_map(
        shards,
        mesh=mesh,
        in_specs=placed,
        out_specs=(
            P("segment", "dp", None, None, "ep", None),
            P("segment", "dp", None, None, None),
        ),
        check_vma=False,
    )
```

time: 623 us -> 61.5 us (0.10)
  the two profiles are of different devices: /device:TPU:8 before, /device:TPU:4 now
where the time goes in v1:
time: 61.5 us; the launch traced here: 61.2 us
  Pallas kernels  57.7 us (94%)
  local copies, waits for them, and re-layouts  2.8 us (5%)
  between operations  0.64 us (1%)
    pallas_call x1, Pallas kernels, shards(): pl.pallas_call(functools.partial(kernel, (nd, ny, nz, nx)), out_shape=(ja...  57.7 us
    reshape x1, local copies, waits for them, and re-layouts, shards(): mix.reshape((1, 1, ny, 2, width))  1.47 us
    reshape x1, local copies, waits for them, and re-layouts, shards(): attention.reshape((1, 1, ny, 2, hl, lat))  1.34 us

profile of v1, /device:TPU:4, one launch (start us, length us, event | category | flops | bytes accessed | tf_op | source)
XLA Modules:
  0.0 61.2 jit_solution(2255554553189063939)
XLA Ops:
  0.6 57.7 %shard_map.131 = (bf16[16,512]{1,0:T(8,128)(2,1)}, bf16[8,3584]{1,0:T(8,128)(2,1)}) custom-call(bf16[2,128,512]{2,1,0:T(8,128)(2,1)} %bitcast.11, bf16[2,576,256]{2,1,0:T(8,128)(2,1)} %bitcast.10, bf16[2,3584,128]{2,1,0:T(8,128)(2,1)} %up_h.1, bf16[2,128,3584]{2,1,0:T(8,128)(2,1)} %dn_h.1, bf16[2,64,128]{2,1,0:T(8,128)(2,1)} %bitcast.12, ...), custom_call_target="tpu_custom_call" | custom-call | tf_op jit(solution)/shard_map/pallas_call | solution.py:395
  58.4 1.3 %reshape.10 = bf16[1,1,4,2,2,512]{5,4,3,2,1,0:T(2,128)(2,1)} reshape(bf16[16,512]{1,0:T(8,128)(2,1)} %get-tuple-element.4) | data formatting | bytes 32768 | tf_op jit(solution)/shard_map/reshape | solution.py:441
  59.7 1.5 %reshape.11 = bf16[1,1,4,2,3584]{4,3,2,1,0:T(2,128)(2,1)} reshape(bf16[8,3584]{1,0:T(8,128)(2,1)} %get-tuple-element.5) | data formatting | bytes 114688 | tf_op jit(solution)/shard_map/reshape | solution.py:442

commit v2 on v1

--- a/solution.py
+++ b/solution.py
@@ -45,10 +45,10 @@
     attn_o, mix_o,
     cv, q, up, dn, tr, nkp, xf, xg,
     a1s, a1r, t1s, t1r, a2s, a2r, a3s, a3r,
-    e1s, e1r, e2s, e2r, e3s, e3r, e4, e4f, e5x, e5y,
+    e1s, e1r, e2s, e2r, e3s, e3r, e5,
     in_sem,
     e0_ss, e0_rs, a1_ss, a1_rs, t1_ss, t1_rs, a2_ss, a2_rs, a3_ss, a3_rs,
-    e1_ss, e1_rs, e2_ss, e2_rs, e3_ss, e3_rs, e4_ss, e4_rs, e5x_ss, e5x_rs, e5y_ss, e5y_rs,
+    e1_ss, e1_rs, e2_ss, e2_rs, e3_ss, e3_rs, e5_ss, e5_rs,
 ):
     nd, ny, nz, nx = sizes
     s, y, ep = lax.axis_index("segment"), lax.axis_index("dp"), lax.axis_index("ep")
@@ -60,8 +60,9 @@
     hl = heads // (nz * nx)
     width = up.shape[1]
     quarter = width // 4
-    ycols = width // ny
-    xcols = e2s.shape[2]
+    nxy = nx * ny
+    spot = y * nx + x
+    block = e2s.shape[2]
     rows_x = a1s.shape[1]
     sec = ny * 4
 
@@ -84,9 +85,10 @@
         to = lax.rem(z + k, nz)
         return to, {"ep": to * nx + x}
 
-    def along_y(k):
-        to = lax.rem(y + k, ny)
-        return to, {"dp": to}
+    def along_xy(k):
+        to_y = lax.rem(y + k // nx, ny)
+        to_x = lax.rem(x + k % nx, nx)
+        return to_y * nx + to_x, {"dp": to_y, "ep": z * nx + to_x}
 
     def across(k):
         to = lax.rem(y + k, ny)
@@ -117,32 +119,21 @@
         return remote(a3s, a3r.at[y], a3_ss, a3_rs, k, across(k)[1])
 
     def c_e1(k):
-        to, dev = plane(k)
-        return remote(e1s.at[to], e1r.at[k], e1_ss, e1_rs, k, dev)
+        return remote(e1s, e1r, e1_ss, e1_rs, k, {"segment": 1 - s})
 
     def c_e2(k):
-        to, dev = along_x(k)
+        to, dev = along_xy(k)
         return remote(e2s.at[to], e2r.at[k], e2_ss, e2_rs, k, dev)
 
     def c_e3(k):
-        to, dev = along_z(k)
-        return remote(e3s.at[to], e3r.at[k], e3_ss, e3_rs, k, dev)
-
-    def c_e4(k):
-        return remote(e4.at[z], e4.at[z], e4_ss, e4_rs, k, along_z(k)[1])
-
-    def c_e5x(k):
-        return remote(e5x.at[x], e5x.at[x], e5x_ss, e5x_rs, k, along_x(k)[1])
-
-    def c_e5y(k):
-        return remote(e5y.at[y], e5y.at[y], e5y_ss, e5y_rs, k, along_y(k)[1])
+        return remote(e3s, e3r.at[k], e3_ss, e3_rs, k, along_z(k)[1])
+
+    def c_e5(k):
+        return remote(e5.at[spot], e5.at[spot], e5_ss, e5_rs, k, along_xy(k)[1])
 
     def each(first, last, act):
-        def body(k, carry):
+        for k in range(first, last):
             act(k)
-            return carry
-
-        lax.fori_loop(first, last, body, 0)
 
     barrier = pltpu.get_barrier_semaphore()
 
@@ -152,9 +143,11 @@
 
         return act
 
+    each(1, nz, greet(along_z))
     each(1, nd, greet(plane))
-    each(1, nx, greet(along_x))
-    each(1, nz, greet(along_z))
+    for k in range(1, nxy):
+        if k % nx:
+            greet(along_xy)(k)
 
     xf[...] = jnp.zeros_like(xf)
     for r in range(2):
@@ -167,9 +160,6 @@
             xf[4 * i + 1:4 * i + 2, quarter:quarter + 8] = gates[r, j:j + 1, :].astype(f32)
             xf[4 * i + 2:4 * i + 3, quarter:] = jnp.full((1, 128), owners[r], jnp.int32).astype(f32)
     xg[d] = xf[...].astype(bf16)
-
-    pl.semaphore_wait(barrier, (nd - 1) + (nx - 1) + (nz - 1))
-    each(1, nd, lambda k: c_e0(k).start())
 
     tr[...] = jnp.zeros_like(tr)
     nkp[...] = jnp.zeros_like(nkp)
@@ -226,60 +216,56 @@
         t1s[to, 0:1, :] = peak[:, to * rows_x:(to + 1) * rows_x]
         t1s[to, 1:2, :] = total[:, to * rows_x:(to + 1) * rows_x]
         t1s[to, 2:8, :] = jnp.zeros((6, rows_x), f32)
+    pl.semaphore_wait(barrier, (nz - 1) + (nd - 1) + (nxy - ny))
+    each(1, nd, lambda k: c_e0(k).start())
     each(1, nx, lambda k: c_t1(k).start())
     each(1, nx, lambda k: c_a1(k).start())
 
-    each(1, nd, lambda k: c_e0(k).wait_recv())
-    loads[2].wait()
-    loads[3].wait()
-    gathered = xg[...].reshape((nd * 16, xg.shape[2]))
-    notes = gathered[:, quarter:]
     row_count = nd * 4
     want = iota((3 * row_count, nd * 16), 0)
     pick = iota((3 * row_count, nd * 16), 1) == 4 * lax.rem(want, row_count) + want // row_count
     pick = jnp.where(pick, 1.0, 0.0).astype(bf16)
+    lane = iota((row_count, 128), 1)
+    experts, hidden_width = up.shape[0], up.shape[2]
+    part_of = lax.rem(iota((nd * 16, experts * hidden_width), 0), 4)
+    loads[2].wait()
+    loads[3].wait()
+    each(1, nd, lambda k: c_e0(k).wait_recv())
+    gathered = xg[...].reshape((nd * 16, xg.shape[2]))
+    acc = jnp.zeros((nd * 16, experts * hidden_width), f32)
+    for part in range(4):
+        weights = jnp.concatenate(
+            [up[e, part * quarter:(part + 1) * quarter, :] for e in range(experts)], axis=1
+        )
+        acc = jnp.where(part_of == part, dot(gathered[:, :quarter], weights), acc)
+    notes = gathered[:, quarter:]
     routing = dot(pick, notes)
     chosen, gate_values = routing[:row_count], routing[row_count:2 * row_count]
-    lane = iota((row_count, 128), 1)
-    part_of = lax.rem(iota((nd * 16, up.shape[2]), 0), 4)
+    acc = acc + pltpu.roll(acc, nd * 16 - 1, 0)
+    acc = acc + pltpu.roll(acc, nd * 16 - 2, 0)
+    hidden = (acc / (1.0 + jnp.exp(-acc))).astype(bf16)
+    hidden = dot(pick[:row_count], hidden).astype(bf16)
     partial = jnp.zeros((row_count, width), f32)
-    for e in range(up.shape[0]):
-        expert = (ep * up.shape[0] + e).astype(f32)
+    for e in range(experts):
+        expert = (ep * experts + e).astype(f32)
         gate = jnp.sum(
             jnp.where((chosen == expert) & (lane < 8), gate_values, 0.0), axis=1, keepdims=True
         )
-        acc = jnp.zeros((nd * 16, up.shape[2]), f32)
-        for part in range(4):
-            piece = dot(gathered[:, :quarter], up[e, part * quarter:(part + 1) * quarter, :])
-            acc = jnp.where(part_of == part, piece, acc)
-        acc = acc + pltpu.roll(acc, nd * 16 - 1, 0)
-        acc = acc + pltpu.roll(acc, nd * 16 - 2, 0)
-        hidden = (acc / (1.0 + jnp.exp(-acc))).astype(bf16)
-        hidden = dot(pick[:row_count], hidden).astype(bf16)
-        partial = partial + gate * dot(hidden, dn[e])
-    for c in range(2):
-        for to in range(ny):
-            e1s[c * ny + to] = partial[
-                (1 - c) * sec:(2 - c) * sec, to * ycols:(to + 1) * ycols
-            ].astype(bf16)
-    each(1, nd, lambda k: c_e1(k).start())
-
-    first_row = jnp.where(s == 0, ny * 16, 0)
-    owner_lane = jnp.where(iota((16, 128), 1) == 0, 1.0, 0.0).astype(bf16)
-
-    def owner_row(count, split):
-        row = iota((count, nd * 16), 0)
-        spot = first_row + 4 * (row // split) + 2
-        pull = jnp.where(iota((count, nd * 16), 1) == spot, 1.0, 0.0).astype(bf16)
-        return dot_rows(owner_lane, dot(pull, notes).astype(bf16))[0:1]
-
-    mine = y.astype(f32)
-    out_i, in_i = iota((2 * ny, sec), 0), iota((2 * ny, sec), 1)
-    mix_pick = (out_i // 2 == in_i // 4) & (lax.rem(out_i, 2) == lax.rem(in_i, 2))
-    mix_pick = jnp.where(mix_pick & (owner_row(sec, 1) == mine), 1.0, 0.0).astype(bf16)
-    out_i, in_i = iota((2 * per // 2 * ny, 2 * per * ny), 0), iota((2 * per // 2 * ny, 2 * per * ny), 1)
-    attn_pick = (out_i // per == in_i // (2 * per)) & (lax.rem(out_i, per) == lax.rem(in_i, per))
-    attn_pick = jnp.where(attn_pick & (owner_row(2 * per * ny, hl) == mine), 1.0, 0.0).astype(bf16)
+        partial = partial + gate * dot(hidden[:, e * hidden_width:(e + 1) * hidden_width], dn[e])
+    first, second = partial[:sec], partial[sec:]
+    e1s[...] = jnp.where(s == 0, first, second).astype(bf16)
+    each(1, 2, lambda k: c_e1(k).start())
+    own = jnp.where(s == 0, second, first)
+
+    each(1, 2, lambda k: c_e1(k).wait_recv())
+    own = own + e1r[...].astype(f32)
+    for to in range(nxy):
+        low, high = to * block, min((to + 1) * block, width)
+        if low < width:
+            e2s[to] = own[:, low:high].astype(bf16)
+        else:
+            e2s[to] = jnp.zeros((sec, block), bf16)
+    each(1, nxy, lambda k: c_e2(k).start())
 
     each(1, nx, lambda k: c_t1(k).wait_recv())
     tops = [t1s[x, 0:1, :]] + [t1r[k, 0:1, :] for k in range(1, nx)]
@@ -299,30 +285,29 @@
     a2s[:, :, lat:] = turned.reshape((nz, 2 * per, 128)).astype(bf16)
     each(1, nz, lambda k: c_a2(k).start())
 
-    each(1, nd, lambda k: c_e1(k).wait_recv())
-    summed = e1s[d].astype(f32)
-    for k in range(1, nd):
-        summed = summed + e1r[k].astype(f32)
-    for to in range(nx):
-        low, high = to * xcols, min((to + 1) * xcols, ycols)
-        e2s[to, :, :high - low] = summed[:, low:high].astype(bf16)
-        if high - low < xcols:
-            e2s[to, :, high - low:] = jnp.zeros((sec, xcols - (high - low)), bf16)
-    each(1, nx, lambda k: c_e2(k).start())
-    each(1, nx, lambda k: c_e2(k).wait_recv())
-    summed = e2s[x].astype(f32)
-    for k in range(1, nx):
+    each(1, nxy, lambda k: c_e2(k).wait_recv())
+    summed = e2s[spot].astype(f32)
+    for k in range(1, nxy):
         summed = summed + e2r[k].astype(f32)
-    rz = sec // nz
-    for to in range(nz):
-        e3s[to] = summed[to * rz:(to + 1) * rz]
+    e3s[...] = summed.astype(bf16)
     each(1, nz, lambda k: c_e3(k).start())
-    each(1, nz, lambda k: c_e3(k).wait_recv())
-    summed = e3s[z]
-    for k in range(1, nz):
-        summed = summed + e3r[k]
-    e4[z] = summed
-    each(1, nz, lambda k: c_e4(k).start())
+
+    first_row = jnp.where(s == 0, ny * 16, 0)
+    owner_lane = jnp.where(iota((16, 128), 1) == 0, 1.0, 0.0).astype(bf16)
+
+    def owner_row(count, split):
+        row = iota((count, nd * 16), 0)
+        source = first_row + 4 * (row // split) + 2
+        pull = jnp.where(iota((count, nd * 16), 1) == source, 1.0, 0.0).astype(bf16)
+        return dot_rows(owner_lane, dot(pull, notes).astype(bf16))[0:1]
+
+    mine = y.astype(f32)
+    out_i, in_i = iota((2 * ny, sec), 0), iota((2 * ny, sec), 1)
+    mix_pick = (out_i // 2 == in_i // 4) & (lax.rem(out_i, 2) == lax.rem(in_i, 2))
+    mix_pick = jnp.where(mix_pick & (owner_row(sec, 1) == mine), 1.0, 0.0).astype(bf16)
+    out_i, in_i = iota((2 * per // 2 * ny, 2 * per * ny), 0), iota((2 * per // 2 * ny, 2 * per * ny), 1)
+    attn_pick = (out_i // per == in_i // (2 * per)) & (lax.rem(out_i, per) == lax.rem(in_i, per))
+    attn_pick = jnp.where(attn_pick & (owner_row(2 * per * ny, hl) == mine), 1.0, 0.0).astype(bf16)
 
     a2r[0] = a2s[z]
     each(1, nz, lambda k: c_a2(k).wait_recv())
@@ -334,39 +319,32 @@
     a3s[...] = (jnp.sum(factors * arrived[:, :, :lat], axis=0) / total).astype(bf16)
     each(0, ny, lambda k: c_a3(k).start())
 
-    each(1, nz, lambda k: c_e4(k).wait_recv())
-    for k in range(nz):
-        e4f[k * rz:(k + 1) * rz, :] = e4[k]
-    e5x[x] = e4f[...].astype(bf16)
-    each(1, nx, lambda k: c_e5x(k).start())
-    each(1, nx, lambda k: c_e5x(k).wait_recv())
-    for k in range(nx):
-        low, high = k * xcols, min((k + 1) * xcols, ycols)
-        e5y[y, :, low:high] = e5x[k, :, :high - low]
-    each(1, ny, lambda k: c_e5y(k).start())
+    each(1, nz, lambda k: c_e3(k).wait_recv())
+    summed = e3s[...].astype(f32)
+    for k in range(1, nz):
+        summed = summed + e3r[k].astype(f32)
+    e5[spot] = summed.astype(bf16)
+    each(1, nxy, lambda k: c_e5(k).start())
 
     each(0, ny, lambda k: c_a3(k).wait_recv())
     finished = a3r[...].astype(f32).reshape((ny * 2 * per, lat)).astype(bf16)
     attn_o[...] = dot(attn_pick, finished).astype(bf16)
-
-    each(1, ny, lambda k: c_e5y(k).wait_recv())
-    for k in range(ny):
-        mix_o[:, k * ycols:(k + 1) * ycols] = dot(mix_pick, e5y[k]).astype(bf16)
-
-    def finish(k, carry):
-        return carry
 
     each(1, nd, lambda k: c_e0(k).wait_send())
     each(1, nx, lambda k: c_t1(k).wait_send())
     each(1, nx, lambda k: c_a1(k).wait_send())
     each(1, nz, lambda k: c_a2(k).wait_send())
     each(0, ny, lambda k: c_a3(k).wait_send())
-    each(1, nd, lambda k: c_e1(k).wait_send())
-    each(1, nx, lambda k: c_e2(k).wait_send())
+    each(1, 2, lambda k: c_e1(k).wait_send())
+    each(1, nxy, lambda k: c_e2(k).wait_send())
     each(1, nz, lambda k: c_e3(k).wait_send())
-    each(1, nz, lambda k: c_e4(k).wait_send())
-    each(1, nx, lambda k: c_e5x(k).wait_send())
-    each(1, ny, lambda k: c_e5y(k).wait_send())
+
+    each(1, nxy, lambda k: c_e5(k).wait_recv())
+    for k in range(nxy):
+        low, high = k * block, min((k + 1) * block, width)
+        if low < width:
+            mix_o[:, low:high] = dot(mix_pick, e5[k]).astype(bf16)
+    each(1, nxy, lambda k: c_e5(k).wait_send())
 
 
 def shards(
@@ -384,8 +362,8 @@
     heads = cols // 2
     hl = heads // (nz * nx)
     width = up_weight.shape[1]
-    ycols = width // ny
-    xcols = -(-ycols // (nx * 128)) * 128
+    nxy = nx * ny
+    block = -(-width // (nxy * 128)) * 128
     sec = ny * 4
     rows_x = nz * 4 * hl
     vmem = pl.BlockSpec(memory_space=pltpu.VMEM)
@@ -417,21 +395,17 @@
             pltpu.VMEM((nz, 4 * hl, lat + 128), bf16),
             pltpu.VMEM((4 * hl, lat), bf16),
             pltpu.VMEM((ny, 4 * hl, lat), bf16),
-            pltpu.VMEM((nd, sec, ycols), bf16),
-            pltpu.VMEM((nd, sec, ycols), bf16),
-            pltpu.VMEM((nx, sec, xcols), bf16),
-            pltpu.VMEM((nx, sec, xcols), bf16),
-            pltpu.VMEM((nz, sec // nz, xcols), f32),
-            pltpu.VMEM((nz, sec // nz, xcols), f32),
-            pltpu.VMEM((nz, sec // nz, xcols), f32),
-            pltpu.VMEM((sec, xcols), f32),
-            pltpu.VMEM((nx, sec, xcols), bf16),
-            pltpu.VMEM((ny, sec, ycols), bf16),
+            pltpu.VMEM((sec, width), bf16),
+            pltpu.VMEM((sec, width), bf16),
+            pltpu.VMEM((nxy, sec, block), bf16),
+            pltpu.VMEM((nxy, sec, block), bf16),
+            pltpu.VMEM((sec, block), bf16),
+            pltpu.VMEM((nz, sec, block), bf16),
+            pltpu.VMEM((nxy, sec, block), bf16),
             sems(4),
             sems(nd), sems(nd), sems(nx), sems(nx), sems(nx), sems(nx), sems(nz), sems(nz),
             sems(ny), sems(ny),
-            sems(nd), sems(nd), sems(nx), sems(nx), sems(nz), sems(nz), sems(nz), sems(nz),
-            sems(nx), sems(nx), sems(ny), sems(ny),
+            sems(2), sems(2), sems(nxy), sems(nxy), sems(nz), sems(nz), sems(nxy), sems(nxy),
         ],
         compiler_params=pltpu.CompilerParams(
             collective_id=0, has_side_effects=True, vmem_limit_bytes=60 * 1024 * 1024

time: 61.5 us -> 50.8 us (0.83)
  the two profiles are of different devices: /device:TPU:4 before, /device:TPU:2 now
where the time goes in v2:
time: 50.8 us; the launch traced here: 50.5 us
  Pallas kernels  47.1 us (93%)
  local copies, waits for them, and re-layouts  2.8 us (6%)
  between operations  0.64 us (1%)
    pallas_call x1, Pallas kernels, shards(): pl.pallas_call(functools.partial(kernel, (nd, ny, nz, nx)), out_shape=(ja...  47.1 us
    reshape x1, local copies, waits for them, and re-layouts, shards(): mix.reshape((1, 1, ny, 2, width))  1.47 us
    reshape x1, local copies, waits for them, and re-layouts, shards(): attention.reshape((1, 1, ny, 2, hl, lat))  1.34 us

profile of v2, /device:TPU:2, one launch (start us, length us, event | category | flops | bytes accessed | tf_op | source)
XLA Modules:
  0.0 50.5 jit_solution(1853102435845680058)
XLA Ops:
  0.6 47.1 %shard_map.131 = (bf16[16,512]{1,0:T(8,128)(2,1)}, bf16[8,3584]{1,0:T(8,128)(2,1)}) custom-call(bf16[2,128,512]{2,1,0:T(8,128)(2,1)} %bitcast.11, bf16[2,576,256]{2,1,0:T(8,128)(2,1)} %bitcast.10, bf16[2,3584,128]{2,1,0:T(8,128)(2,1)} %up_h.1, bf16[2,128,3584]{2,1,0:T(8,128)(2,1)} %dn_h.1, bf16[2,64,128]{2,1,0:T(8,128)(2,1)} %bitcast.12, ...), custom_call_target="tpu_custom_call" | custom-call | tf_op jit(solution)/shard_map/pallas_call | solution.py:373
  47.7 1.3 %reshape.10 = bf16[1,1,4,2,2,512]{5,4,3,2,1,0:T(2,128)(2,1)} reshape(bf16[16,512]{1,0:T(8,128)(2,1)} %get-tuple-element.4) | data formatting | bytes 32768 | tf_op jit(solution)/shard_map/reshape | solution.py:415
  49.1 1.5 %reshape.11 = bf16[1,1,4,2,3584]{4,3,2,1,0:T(2,128)(2,1)} reshape(bf16[8,3584]{1,0:T(8,128)(2,1)} %get-tuple-element.5) | data formatting | bytes 114688 | tf_op jit(solution)/shard_map/reshape | solution.py:416

commit v3 on v2

--- a/solution.py
+++ b/solution.py
@@ -41,9 +41,9 @@
 
 def kernel(
     sizes,
-    cv_h, q_h, up_h, dn_h, cr, cs, nk, xr, ids, gates, owners, lengths,
+    cv_h, q_h, up_h, dn_h, cr_h, cs_h, nk_h, xr_h, ids_h, gates_h, owners_h, lengths_h,
     attn_o, mix_o,
-    cv, q, up, dn, tr, nkp, xf, xg,
+    cv, q, up, dn, cr, cs, nk, xr, ids, gates, owners, lengths, tr, nkp, xf, xg,
     a1s, a1r, t1s, t1r, a2s, a2r, a3s, a3r,
     e1s, e1r, e2s, e2r, e3s, e3r, e5,
     in_sem,
@@ -60,35 +60,35 @@
     hl = heads // (nz * nx)
     width = up.shape[1]
     quarter = width // 4
-    nxy = nx * ny
-    spot = y * nx + x
+    pair, side, pairs = z // 2, lax.rem(z, 2), nz // 2
+    corner = x * 2 + side
+    corners = nx * 2
+    spot = y * corners + corner
+    spots = ny * corners
     block = e2s.shape[2]
     rows_x = a1s.shape[1]
     sec = ny * 4
 
-    loads = [
-        pltpu.make_async_copy(a, b, in_sem.at[i])
-        for i, (a, b) in enumerate(((cv_h, cv), (q_h, q), (up_h, up), (dn_h, dn)))
-    ]
-    for load in loads:
-        load.start()
-
     def plane(k):
         to = lax.rem(d + k, nd)
         return to, {"segment": to // ny, "dp": lax.rem(to, ny)}
 
-    def along_x(k):
-        to = lax.rem(x + k, nx)
-        return to, {"ep": z * nx + to}
-
-    def along_z(k):
-        to = lax.rem(z + k, nz)
-        return to, {"ep": to * nx + x}
-
-    def along_xy(k):
-        to_y = lax.rem(y + k // nx, ny)
-        to_x = lax.rem(x + k % nx, nx)
-        return to_y * nx + to_x, {"dp": to_y, "ep": z * nx + to_x}
+    def near(k):
+        to_x = lax.rem(x + k // 2, nx)
+        to_side = lax.rem(side + k % 2, 2)
+        return to_x * 2 + to_side, {"ep": (pair * 2 + to_side) * nx + to_x}
+
+    def both_planes(k):
+        to_y = lax.rem(y + k // corners, ny)
+        to_x = lax.rem(x + (k // 2) % nx, nx)
+        to_side = lax.rem(side + k % 2, 2)
+        return (to_y * nx + to_x) * 2 + to_side, {
+            "dp": to_y, "ep": (pair * 2 + to_side) * nx + to_x,
+        }
+
+    def far(k):
+        to = lax.rem(pair + k, pairs)
+        return to, {"ep": (to * 2 + side) * nx + x}
 
     def across(k):
         to = lax.rem(y + k, ny)
@@ -104,15 +104,15 @@
         return remote(xg.at[d], xg.at[d], e0_ss, e0_rs, k, plane(k)[1])
 
     def c_a1(k):
-        to, dev = along_x(k)
+        to, dev = near(k)
         return remote(a1s.at[to], a1r.at[k], a1_ss, a1_rs, k, dev)
 
     def c_t1(k):
-        to, dev = along_x(k)
+        to, dev = near(k)
         return remote(t1s.at[to], t1r.at[k], t1_ss, t1_rs, k, dev)
 
     def c_a2(k):
-        to, dev = along_z(k)
+        to, dev = far(k)
         return remote(a2s.at[to], a2r.at[k], a2_ss, a2_rs, k, dev)
 
     def c_a3(k):
@@ -122,14 +122,14 @@
         return remote(e1s, e1r, e1_ss, e1_rs, k, {"segment": 1 - s})
 
     def c_e2(k):
-        to, dev = along_xy(k)
+        to, dev = both_planes(k)
         return remote(e2s.at[to], e2r.at[k], e2_ss, e2_rs, k, dev)
 
     def c_e3(k):
-        return remote(e3s, e3r.at[k], e3_ss, e3_rs, k, along_z(k)[1])
+        return remote(e3s, e3r.at[k], e3_ss, e3_rs, k, far(k)[1])
 
     def c_e5(k):
-        return remote(e5.at[spot], e5.at[spot], e5_ss, e5_rs, k, along_xy(k)[1])
+        return remote(e5.at[spot], e5.at[spot], e5_ss, e5_rs, k, both_planes(k)[1])
 
     def each(first, last, act):
         for k in range(first, last):
@@ -143,13 +143,24 @@
 
         return act
 
-    each(1, nz, greet(along_z))
+    each(1, pairs, greet(far))
     each(1, nd, greet(plane))
-    for k in range(1, nxy):
-        if k % nx:
-            greet(along_xy)(k)
+    for k in range(1, spots):
+        if k % corners:
+            greet(both_planes)(k)
+
+    loads = {}
+    for n, (name, src, dst) in enumerate((
+        ("rows", xr_h, xr), ("ids", ids_h, ids), ("gates", gates_h, gates), ("owners", owners_h, owners),
+        ("values", cv_h, cv), ("scales", cs_h, cs), ("queries", q_h, q), ("rope", cr_h, cr),
+        ("fresh", nk_h, nk), ("lengths", lengths_h, lengths), ("up", up_h, up), ("down", dn_h, dn),
+    )):
+        loads[name] = pltpu.make_async_copy(src, dst, in_sem.at[n])
+        loads[name].start()
 
     xf[...] = jnp.zeros_like(xf)
+    for name in ("rows", "ids", "gates", "owners"):
+        loads[name].wait()
     for r in range(2):
         for j in range(2):
             i = 2 * r + j
@@ -163,21 +174,25 @@
 
     tr[...] = jnp.zeros_like(tr)
     nkp[...] = jnp.zeros_like(nkp)
+    loads["scales"].wait()
+    loads["fresh"].wait()
     for r in range(2):
         tr[8 * r:8 * r + 4, :ctx] = cs[r].astype(f32)
         nkp[16 * r:16 * r + 2, :] = nk[r].astype(f32)
     scale_cols = tr[:, :ctx].T
-    total_rows = nx * rows_x
+    total_rows = corners * rows_x
     place = iota((total_rows, cols), 0)
     per = 2 * hl
     h_of = lax.rem(place, hl)
     j_of = lax.rem(place // hl, 2)
     r_of = lax.rem(place // per, 2)
-    z_of = lax.rem(place // (2 * per), nz)
-    x_of = place // (2 * per * nz)
+    pair_of = lax.rem(place // (2 * per), pairs)
+    side_of = lax.rem(place // (2 * per * pairs), 2)
+    x_of = place // (4 * per * pairs)
+    z_of = pair_of * 2 + side_of
     match = (j_of * heads + (z_of * nx + x_of) * hl + h_of) == iota((total_rows, cols), 1)
-    loads[0].wait()
-    loads[1].wait()
+    for name in ("values", "queries", "rope", "lengths"):
+        loads[name].wait()
     out = jnp.zeros((total_rows, lat), f32)
     stats = jnp.zeros((16, total_rows), f32)
     for r in range(2):
@@ -209,17 +224,17 @@
         out = out + dot(dot_rows(order, cached.astype(bf16)).astype(bf16), latent)
         out = out + dot(dot_rows(order, newer.astype(bf16)).astype(bf16), fresh[:, :lat])
         stats = stats + dot_rows(extra.astype(bf16), order)
+    t1s[...] = jnp.zeros_like(t1s)
     peak = stats[0:1] + stats[1:2] + stats[2:3]
     total = stats[3:4] + stats[4:5] + stats[5:6]
-    for to in range(nx):
+    for to in range(corners):
         a1s[to] = out[to * rows_x:(to + 1) * rows_x].astype(bf16)
-        t1s[to, 0:1, :] = peak[:, to * rows_x:(to + 1) * rows_x]
-        t1s[to, 1:2, :] = total[:, to * rows_x:(to + 1) * rows_x]
-        t1s[to, 2:8, :] = jnp.zeros((6, rows_x), f32)
-    pl.semaphore_wait(barrier, (nz - 1) + (nd - 1) + (nxy - ny))
+        t1s[to, 0:1, :rows_x] = peak[:, to * rows_x:(to + 1) * rows_x]
+        t1s[to, 1:2, :rows_x] = total[:, to * rows_x:(to + 1) * rows_x]
+    pl.semaphore_wait(barrier, (pairs - 1) + (nd - 1) + (spots - ny))
     each(1, nd, lambda k: c_e0(k).start())
-    each(1, nx, lambda k: c_t1(k).start())
-    each(1, nx, lambda k: c_a1(k).start())
+    each(1, corners, lambda k: c_t1(k).start())
+    each(1, corners, lambda k: c_a1(k).start())
 
     row_count = nd * 4
     want = iota((3 * row_count, nd * 16), 0)
@@ -228,8 +243,8 @@
     lane = iota((row_count, 128), 1)
     experts, hidden_width = up.shape[0], up.shape[2]
     part_of = lax.rem(iota((nd * 16, experts * hidden_width), 0), 4)
-    loads[2].wait()
-    loads[3].wait()
+    loads["up"].wait()
+    loads["down"].wait()
     each(1, nd, lambda k: c_e0(k).wait_recv())
     gathered = xg[...].reshape((nd * 16, xg.shape[2]))
     acc = jnp.zeros((nd * 16, experts * hidden_width), f32)
@@ -259,38 +274,38 @@
 
     each(1, 2, lambda k: c_e1(k).wait_recv())
     own = own + e1r[...].astype(f32)
-    for to in range(nxy):
+    for to in range(spots):
         low, high = to * block, min((to + 1) * block, width)
         if low < width:
             e2s[to] = own[:, low:high].astype(bf16)
         else:
             e2s[to] = jnp.zeros((sec, block), bf16)
-    each(1, nxy, lambda k: c_e2(k).start())
-
-    each(1, nx, lambda k: c_t1(k).wait_recv())
-    tops = [t1s[x, 0:1, :]] + [t1r[k, 0:1, :] for k in range(1, nx)]
-    sums = [t1s[x, 1:2, :]] + [t1r[k, 1:2, :] for k in range(1, nx)]
+    each(1, spots, lambda k: c_e2(k).start())
+
+    each(1, corners, lambda k: c_t1(k).wait_recv())
+    tops = [t1s[corner, 0:1, :rows_x]] + [t1r[k, 0:1, :rows_x] for k in range(1, corners)]
+    sums = [t1s[corner, 1:2, :rows_x]] + [t1r[k, 1:2, :rows_x] for k in range(1, corners)]
     top = functools.reduce(jnp.maximum, tops)
     factors = [jnp.exp(one - top) for one in tops]
     total = functools.reduce(jnp.add, [a * b for a, b in zip(factors, sums)])
     tr[...] = jnp.zeros_like(tr)
     for n, one in enumerate(list(three_parts(top) + three_parts(total)) + factors):
         tr[n:n + 1, :rows_x] = one
-    turned = tr[:, :rows_x].T
-    each(1, nx, lambda k: c_a1(k).wait_recv())
-    merged = turned[:, 6:7] * a1s[x].astype(f32)
-    for k in range(1, nx):
+    turned = tr[...].T[:rows_x]
+    each(1, corners, lambda k: c_a1(k).wait_recv())
+    merged = turned[:, 6:7] * a1s[corner].astype(f32)
+    for k in range(1, corners):
         merged = merged + turned[:, 6 + k:7 + k] * a1r[k].astype(f32)
-    a2s[:, :, :lat] = merged.reshape((nz, 2 * per, lat)).astype(bf16)
-    a2s[:, :, lat:] = turned.reshape((nz, 2 * per, 128)).astype(bf16)
-    each(1, nz, lambda k: c_a2(k).start())
-
-    each(1, nxy, lambda k: c_e2(k).wait_recv())
+    a2s[:, :, :lat] = merged.reshape((pairs, 2 * per, lat)).astype(bf16)
+    a2s[:, :, lat:] = turned.reshape((pairs, 2 * per, 128)).astype(bf16)
+    each(1, pairs, lambda k: c_a2(k).start())
+
+    each(1, spots, lambda k: c_e2(k).wait_recv())
     summed = e2s[spot].astype(f32)
-    for k in range(1, nxy):
+    for k in range(1, spots):
         summed = summed + e2r[k].astype(f32)
     e3s[...] = summed.astype(bf16)
-    each(1, nz, lambda k: c_e3(k).start())
+    each(1, pairs, lambda k: c_e3(k).start())
 
     first_row = jnp.where(s == 0, ny * 16, 0)
     owner_lane = jnp.where(iota((16, 128), 1) == 0, 1.0, 0.0).astype(bf16)
@@ -309,8 +324,8 @@
     attn_pick = (out_i // per == in_i // (2 * per)) & (lax.rem(out_i, per) == lax.rem(in_i, per))
     attn_pick = jnp.where(attn_pick & (owner_row(2 * per * ny, hl) == mine), 1.0, 0.0).astype(bf16)
 
-    a2r[0] = a2s[z]
-    each(1, nz, lambda k: c_a2(k).wait_recv())
+    a2r[0] = a2s[pair]
+    each(1, pairs, lambda k: c_a2(k).wait_recv())
     arrived = a2r[...].astype(f32)
     tops = arrived[:, :, lat:lat + 1] + arrived[:, :, lat + 1:lat + 2] + arrived[:, :, lat + 2:lat + 3]
     sums = arrived[:, :, lat + 3:lat + 4] + arrived[:, :, lat + 4:lat + 5] + arrived[:, :, lat + 5:lat + 6]
@@ -319,32 +334,32 @@
     a3s[...] = (jnp.sum(factors * arrived[:, :, :lat], axis=0) / total).astype(bf16)
     each(0, ny, lambda k: c_a3(k).start())
 
-    each(1, nz, lambda k: c_e3(k).wait_recv())
+    each(1, pairs, lambda k: c_e3(k).wait_recv())
     summed = e3s[...].astype(f32)
-    for k in range(1, nz):
+    for k in range(1, pairs):
         summed = summed + e3r[k].astype(f32)
     e5[spot] = summed.astype(bf16)
-    each(1, nxy, lambda k: c_e5(k).start())
+    each(1, spots, lambda k: c_e5(k).start())
 
     each(0, ny, lambda k: c_a3(k).wait_recv())
     finished = a3r[...].astype(f32).reshape((ny * 2 * per, lat)).astype(bf16)
     attn_o[...] = dot(attn_pick, finished).astype(bf16)
 
     each(1, nd, lambda k: c_e0(k).wait_send())
-    each(1, nx, lambda k: c_t1(k).wait_send())
-    each(1, nx, lambda k: c_a1(k).wait_send())
-    each(1, nz, lambda k: c_a2(k).wait_send())
+    each(1, corners, lambda k: c_t1(k).wait_send())
+    each(1, corners, lambda k: c_a1(k).wait_send())
+    each(1, pairs, lambda k: c_a2(k).wait_send())
     each(0, ny, lambda k: c_a3(k).wait_send())
     each(1, 2, lambda k: c_e1(k).wait_send())
-    each(1, nxy, lambda k: c_e2(k).wait_send())
-    each(1, nz, lambda k: c_e3(k).wait_send())
-
-    each(1, nxy, lambda k: c_e5(k).wait_recv())
-    for k in range(nxy):
+    each(1, spots, lambda k: c_e2(k).wait_send())
+    each(1, pairs, lambda k: c_e3(k).wait_send())
+
+    each(1, spots, lambda k: c_e5(k).wait_recv())
+    for k in range(spots):
         low, high = k * block, min((k + 1) * block, width)
         if low < width:
             mix_o[:, low:high] = dot(mix_pick, e5[k]).astype(bf16)
-    each(1, nxy, lambda k: c_e5(k).wait_send())
+    each(1, spots, lambda k: c_e5(k).wait_send())
 
 
 def shards(
@@ -362,12 +377,12 @@
     heads = cols // 2
     hl = heads // (nz * nx)
     width = up_weight.shape[1]
-    nxy = nx * ny
-    block = -(-width // (nxy * 128)) * 128
+    corners, pairs = nx * 2, nz // 2
+    spots = ny * corners
+    block = -(-width // (spots * 128)) * 128
     sec = ny * 4
-    rows_x = nz * 4 * hl
+    rows_x = pairs * 4 * hl
     vmem = pl.BlockSpec(memory_space=pltpu.VMEM)
-    smem = pl.BlockSpec(memory_space=pltpu.SMEM)
     anywhere = pl.BlockSpec(memory_space=pl.ANY)
     sems = lambda n: pltpu.SemaphoreType.DMA((n,))
     attention, mix = pl.pallas_call(
@@ -376,36 +391,44 @@
             jax.ShapeDtypeStruct((ny * 2 * hl, lat), bf16),
             jax.ShapeDtypeStruct((ny * 2, width), bf16),
         ),
-        in_specs=[anywhere] * 4 + [vmem] * 6 + [smem] * 2,
+        in_specs=[anywhere] * 12,
         out_specs=(vmem, vmem),
         scratch_shapes=[
             pltpu.VMEM(cv.shape, bf16),
             pltpu.VMEM(q.shape, bf16),
             pltpu.VMEM(up_weight.shape, bf16),
             pltpu.VMEM(down_weight.shape, bf16),
+            pltpu.VMEM(cr.shape, bf16),
+            pltpu.VMEM(cs.shape, bf16),
+            pltpu.VMEM(nk.shape, bf16),
+            pltpu.VMEM(xr.shape, bf16),
+            pltpu.VMEM(ids.shape, jnp.int32),
+            pltpu.VMEM(gates.shape, bf16),
+            pltpu.SMEM(owners[0, 0].shape, jnp.int32),
+            pltpu.SMEM(lengths[0, 0].shape, jnp.int32),
             pltpu.VMEM((128, 128), f32),
             pltpu.VMEM((32, nk.shape[2]), f32),
             pltpu.VMEM((16, width // 4 + 128), f32),
             pltpu.VMEM((nd, 16, width // 4 + 128), bf16),
-            pltpu.VMEM((nx, rows_x, lat), bf16),
-            pltpu.VMEM((nx, rows_x, lat), bf16),
-            pltpu.VMEM((nx, 8, rows_x), f32),
-            pltpu.VMEM((nx, 8, rows_x), f32),
-            pltpu.VMEM((nz, 4 * hl, lat + 128), bf16),
-            pltpu.VMEM((nz, 4 * hl, lat + 128), bf16),
+            pltpu.VMEM((corners, rows_x, lat), bf16),
+            pltpu.VMEM((corners, rows_x, lat), bf16),
+            pltpu.VMEM((corners, 8, 128), f32),
+            pltpu.VMEM((corners, 8, 128), f32),
+            pltpu.VMEM((pairs, 4 * hl, lat + 128), bf16),
+            pltpu.VMEM((pairs, 4 * hl, lat + 128), bf16),
             pltpu.VMEM((4 * hl, lat), bf16),
             pltpu.VMEM((ny, 4 * hl, lat), bf16),
             pltpu.VMEM((sec, width), bf16),
             pltpu.VMEM((sec, width), bf16),
-            pltpu.VMEM((nxy, sec, block), bf16),
-            pltpu.VMEM((nxy, sec, block), bf16),
+            pltpu.VMEM((spots, sec, block), bf16),
+            pltpu.VMEM((spots, sec, block), bf16),
             pltpu.VMEM((sec, block), bf16),
-            pltpu.VMEM((nz, sec, block), bf16),
-            pltpu.VMEM((nxy, sec, block), bf16),
-            sems(4),
-            sems(nd), sems(nd), sems(nx), sems(nx), sems(nx), sems(nx), sems(nz), sems(nz),
-            sems(ny), sems(ny),
-            sems(2), sems(2), sems(nxy), sems(nxy), sems(nz), sems(nz), sems(nxy), sems(nxy),
+            pltpu.VMEM((pairs, sec, block), bf16),
+            pltpu.VMEM((spots, sec, block), bf16),
+            sems(12),
+            sems(nd), sems(nd), sems(corners), sems(corners), sems(corners), sems(corners),
+            sems(pairs), sems(pairs), sems(ny), sems(ny),
+            sems(2), sems(2), sems(spots), sems(spots), sems(pairs), sems(pairs), sems(spots), sems(spots),
         ],
         compiler_params=pltpu.CompilerParams(
             collective_id=0, has_side_effects=True, vmem_limit_bytes=60 * 1024 * 1024

time: 50.8 us -> 47.1 us (0.927)
  the two profiles are of different devices: /device:TPU:2 before, /device:TPU:32 now
where the time goes in v3:
time: 47.1 us; the launch traced here: 46.9 us
  Pallas kernels  43.5 us (92%)
  local copies, waits for them, and re-layouts  2.8 us (6%)
  between operations  0.64 us (1%)
    pallas_call x1, Pallas kernels, shards(): pl.pallas_call(functools.partial(kernel, (nd, ny, nz, nx)), out_shape=(ja...  43.5 us
    reshape x1, local copies, waits for them, and re-layouts, shards(): mix.reshape((1, 1, ny, 2, width))  1.47 us
    reshape x1, local copies, waits for them, and re-layouts, shards(): attention.reshape((1, 1, ny, 2, hl, lat))  1.34 us

profile of v3, /device:TPU:32, one launch (start us, length us, event | category | flops | bytes accessed | tf_op | source)
XLA Modules:
  0.0 46.9 jit_solution(465997165000800977)
XLA Ops:
  0.6 43.5 %shard_map.131 = (bf16[16,512]{1,0:T(8,128)(2,1)}, bf16[8,3584]{1,0:T(8,128)(2,1)}) custom-call(bf16[2,128,512]{2,1,0:T(8,128)(2,1)} %bitcast.11, bf16[2,576,256]{2,1,0:T(8,128)(2,1)} %bitcast.10, bf16[2,3584,128]{2,1,0:T(8,128)(2,1)} %up_h.1, bf16[2,128,3584]{2,1,0:T(8,128)(2,1)} %dn_h.1, bf16[2,64,128]{2,1,0:T(8,128)(2,1)} %bitcast.12, ...), custom_call_target="tpu_custom_call" | custom-call | tf_op jit(solution)/shard_map/pallas_call | solution.py:388
  44.1 1.3 %reshape.10 = bf16[1,1,4,2,2,512]{5,4,3,2,1,0:T(2,128)(2,1)} reshape(bf16[16,512]{1,0:T(8,128)(2,1)} %get-tuple-element.4) | data formatting | bytes 32768 | tf_op jit(solution)/shard_map/reshape | solution.py:438
  45.4 1.5 %reshape.11 = bf16[1,1,4,2,3584]{4,3,2,1,0:T(2,128)(2,1)} reshape(bf16[8,3584]{1,0:T(8,128)(2,1)} %get-tuple-element.5) | data formatting | bytes 114688 | tf_op jit(solution)/shard_map/reshape | solution.py:439

commit v4 on v3

--- a/solution.py
+++ b/solution.py
@@ -65,7 +65,8 @@
     corners = nx * 2
     spot = y * corners + corner
     spots = ny * corners
-    block = e2s.shape[2]
+    block = e2s.shape[3]
+    strip = corners * block
     rows_x = a1s.shape[1]
     sec = ny * 4
 
@@ -119,11 +120,11 @@
         return remote(a3s, a3r.at[y], a3_ss, a3_rs, k, across(k)[1])
 
     def c_e1(k):
-        return remote(e1s, e1r, e1_ss, e1_rs, k, {"segment": 1 - s})
+        return remote(e1s.at[k], e1r.at[k], e1_ss, e1_rs, k, {"segment": 1 - s})
 
     def c_e2(k):
         to, dev = both_planes(k)
-        return remote(e2s.at[to], e2r.at[k], e2_ss, e2_rs, k, dev)
+        return remote(e2s.at[k // corners, lax.rem(to, corners)], e2r.at[k], e2_ss, e2_rs, k, dev)
 
     def c_e3(k):
         return remote(e3s, e3r.at[k], e3_ss, e3_rs, k, far(k)[1])
@@ -135,6 +136,25 @@
         for k in range(first, last):
             act(k)
 
+    def ring(k, n):
+        return min(k % n, -k % n)
+
+    def farthest(first, last, hops):
+        return sorted(range(first, last), key=lambda k: -hops(k))
+
+    plane_order = farthest(1, nd, lambda k: ring(k, ny) if k % ny else 0.5)
+    near_order = farthest(1, corners, lambda k: ring(k // 2, nx) + k % 2)
+    far_order = farthest(1, pairs, lambda k: ring(k, pairs))
+    strips = farthest(0, ny, lambda k: ring(k, ny))
+    corner_order = farthest(0, corners, lambda k: ring(k // 2, nx) + k % 2)
+    spot_order = farthest(
+        1, spots, lambda k: ring(k // corners, ny) + ring((k % corners) // 2, nx) + k % 2
+    )
+
+    def start(copy, order):
+        for k in order:
+            copy(k).start()
+
     barrier = pltpu.get_barrier_semaphore()
 
     def greet(where):
@@ -143,8 +163,8 @@
 
         return act
 
+    each(1, nd, greet(plane))
     each(1, pairs, greet(far))
-    each(1, nd, greet(plane))
     for k in range(1, spots):
         if k % corners:
             greet(both_planes)(k)
@@ -153,7 +173,7 @@
     for n, (name, src, dst) in enumerate((
         ("rows", xr_h, xr), ("ids", ids_h, ids), ("gates", gates_h, gates), ("owners", owners_h, owners),
         ("values", cv_h, cv), ("scales", cs_h, cs), ("queries", q_h, q), ("rope", cr_h, cr),
-        ("fresh", nk_h, nk), ("lengths", lengths_h, lengths), ("up", up_h, up), ("down", dn_h, dn),
+        ("fresh", nk_h, nk), ("lengths", lengths_h, lengths), ("up", up_h, up), ("down", dn_h, dn.at[:, :, :width]),
     )):
         loads[name] = pltpu.make_async_copy(src, dst, in_sem.at[n])
         loads[name].start()
@@ -232,9 +252,9 @@
         t1s[to, 0:1, :rows_x] = peak[:, to * rows_x:(to + 1) * rows_x]
         t1s[to, 1:2, :rows_x] = total[:, to * rows_x:(to + 1) * rows_x]
     pl.semaphore_wait(barrier, (pairs - 1) + (nd - 1) + (spots - ny))
-    each(1, nd, lambda k: c_e0(k).start())
-    each(1, corners, lambda k: c_t1(k).start())
-    each(1, corners, lambda k: c_a1(k).start())
+    start(c_e0, plane_order)
+    start(c_t1, near_order)
+    start(c_a1, near_order)
 
     row_count = nd * 4
     want = iota((3 * row_count, nd * 16), 0)
@@ -242,6 +262,8 @@
     pick = jnp.where(pick, 1.0, 0.0).astype(bf16)
     lane = iota((row_count, 128), 1)
     experts, hidden_width = up.shape[0], up.shape[2]
+    if dn.shape[2] > width:
+        dn[:, :, width:] = jnp.zeros((experts, hidden_width, dn.shape[2] - width), bf16)
     part_of = lax.rem(iota((nd * 16, experts * hidden_width), 0), 4)
     loads["up"].wait()
     loads["down"].wait()
@@ -260,27 +282,30 @@
     acc = acc + pltpu.roll(acc, nd * 16 - 2, 0)
     hidden = (acc / (1.0 + jnp.exp(-acc))).astype(bf16)
     hidden = dot(pick[:row_count], hidden).astype(bf16)
-    partial = jnp.zeros((row_count, width), f32)
+    hiddens, expert_gates = [], []
     for e in range(experts):
         expert = (ep * experts + e).astype(f32)
-        gate = jnp.sum(
+        expert_gates.append(jnp.sum(
             jnp.where((chosen == expert) & (lane < 8), gate_values, 0.0), axis=1, keepdims=True
-        )
-        partial = partial + gate * dot(hidden[:, e * hidden_width:(e + 1) * hidden_width], dn[e])
-    first, second = partial[:sec], partial[sec:]
-    e1s[...] = jnp.where(s == 0, first, second).astype(bf16)
-    each(1, 2, lambda k: c_e1(k).start())
-    own = jnp.where(s == 0, second, first)
-
-    each(1, 2, lambda k: c_e1(k).wait_recv())
-    own = own + e1r[...].astype(f32)
-    for to in range(spots):
-        low, high = to * block, min((to + 1) * block, width)
-        if low < width:
-            e2s[to] = own[:, low:high].astype(bf16)
-        else:
-            e2s[to] = jnp.zeros((sec, block), bf16)
-    each(1, spots, lambda k: c_e2(k).start())
+        ))
+        hiddens.append(hidden[:, e * hidden_width:(e + 1) * hidden_width])
+    owns = {}
+    for j in strips:
+        low = pl.multiple_of(lax.rem(y + j, ny) * strip, 128)
+        partial = jnp.zeros((row_count, strip), f32)
+        for e in range(experts):
+            partial = partial + expert_gates[e] * dot(hiddens[e], dn[e, :, pl.ds(low, strip)])
+        first, second = partial[:sec], partial[sec:]
+        e1s[j] = jnp.where(s == 0, first, second).astype(bf16)
+        c_e1(j).start()
+        owns[j] = jnp.where(s == 0, second, first)
+
+    for j in strips:
+        c_e1(j).wait_recv()
+        own = owns[j] + e1r[j].astype(f32)
+        for to in range(corners):
+            e2s[j, to] = own[:, to * block:(to + 1) * block].astype(bf16)
+        start(c_e2, [k for k in (j * corners + c for c in corner_order) if k])
 
     each(1, corners, lambda k: c_t1(k).wait_recv())
     tops = [t1s[corner, 0:1, :rows_x]] + [t1r[k, 0:1, :rows_x] for k in range(1, corners)]
@@ -298,14 +323,14 @@
         merged = merged + turned[:, 6 + k:7 + k] * a1r[k].astype(f32)
     a2s[:, :, :lat] = merged.reshape((pairs, 2 * per, lat)).astype(bf16)
     a2s[:, :, lat:] = turned.reshape((pairs, 2 * per, 128)).astype(bf16)
-    each(1, pairs, lambda k: c_a2(k).start())
+    start(c_a2, far_order)
 
     each(1, spots, lambda k: c_e2(k).wait_recv())
-    summed = e2s[spot].astype(f32)
+    summed = e2s[0, corner].astype(f32)
     for k in range(1, spots):
         summed = summed + e2r[k].astype(f32)
     e3s[...] = summed.astype(bf16)
-    each(1, pairs, lambda k: c_e3(k).start())
+    start(c_e3, far_order)
 
     first_row = jnp.where(s == 0, ny * 16, 0)
     owner_lane = jnp.where(iota((16, 128), 1) == 0, 1.0, 0.0).astype(bf16)
@@ -332,14 +357,14 @@
     factors = jnp.exp(tops - jnp.max(tops, axis=0, keepdims=True))
     total = jnp.sum(factors * sums, axis=0)
     a3s[...] = (jnp.sum(factors * arrived[:, :, :lat], axis=0) / total).astype(bf16)
-    each(0, ny, lambda k: c_a3(k).start())
+    start(c_a3, strips)
 
     each(1, pairs, lambda k: c_e3(k).wait_recv())
     summed = e3s[...].astype(f32)
     for k in range(1, pairs):
         summed = summed + e3r[k].astype(f32)
     e5[spot] = summed.astype(bf16)
-    each(1, spots, lambda k: c_e5(k).start())
+    start(c_e5, spot_order)
 
     each(0, ny, lambda k: c_a3(k).wait_recv())
     finished = a3r[...].astype(f32).reshape((ny * 2 * per, lat)).astype(bf16)
@@ -350,7 +375,7 @@
     each(1, corners, lambda k: c_a1(k).wait_send())
     each(1, pairs, lambda k: c_a2(k).wait_send())
     each(0, ny, lambda k: c_a3(k).wait_send())
-    each(1, 2, lambda k: c_e1(k).wait_send())
+    each(0, ny, lambda k: c_e1(k).wait_send())
     each(1, spots, lambda k: c_e2(k).wait_send())
     each(1, pairs, lambda k: c_e3(k).wait_send())
 
@@ -360,6 +385,16 @@
         if low < width:
             mix_o[:, low:high] = dot(mix_pick, e5[k]).astype(bf16)
     each(1, spots, lambda k: c_e5(k).wait_send())
+
+
+def placed_kernel(attention, mix, attn_o, mix_o):
+    ny, hl = attn_o.shape[2], attn_o.shape[4]
+    attended, mixed = attention[...].astype(f32), mix[...].astype(f32)
+    for g in range(ny):
+        mix_o[0, 0, g] = mixed[2 * g:2 * g + 2].astype(bf16)
+        for j in range(2):
+            low = (2 * g + j) * hl
+            attn_o[0, 0, g, j] = attended[low:low + hl].astype(bf16)
 
 
 def shards(
@@ -397,7 +432,7 @@
             pltpu.VMEM(cv.shape, bf16),
             pltpu.VMEM(q.shape, bf16),
             pltpu.VMEM(up_weight.shape, bf16),
-            pltpu.VMEM(down_weight.shape, bf16),
+            pltpu.VMEM(down_weight.shape[:2] + (spots * block,), bf16),
             pltpu.VMEM(cr.shape, bf16),
             pltpu.VMEM(cs.shape, bf16),
             pltpu.VMEM(nk.shape, bf16),
@@ -418,9 +453,9 @@
             pltpu.VMEM((pairs, 4 * hl, lat + 128), bf16),
             pltpu.VMEM((4 * hl, lat), bf16),
             pltpu.VMEM((ny, 4 * hl, lat), bf16),
-            pltpu.VMEM((sec, width), bf16),
-            pltpu.VMEM((sec, width), bf16),
-            pltpu.VMEM((spots, sec, block), bf16),
+            pltpu.VMEM((ny, sec, corners * block), bf16),
+            pltpu.VMEM((ny, sec, corners * block), bf16),
+            pltpu.VMEM((ny, corners, sec, block), bf16),
             pltpu.VMEM((spots, sec, block), bf16),
             pltpu.VMEM((sec, block), bf16),
             pltpu.VMEM((pairs, sec, block), bf16),
@@ -428,16 +463,21 @@
             sems(12),
             sems(nd), sems(nd), sems(corners), sems(corners), sems(corners), sems(corners),
             sems(pairs), sems(pairs), sems(ny), sems(ny),
-            sems(2), sems(2), sems(spots), sems(spots), sems(pairs), sems(pairs), sems(spots), sems(spots),
+            sems(ny), sems(ny), sems(spots), sems(spots), sems(pairs), sems(pairs), sems(spots), sems(spots),
         ],
         compiler_params=pltpu.CompilerParams(
             collective_id=0, has_side_effects=True, vmem_limit_bytes=60 * 1024 * 1024
         ),
     )(cv, q, up_weight, down_weight, cr, cs, nk, xr, ids, gates, owners[0, 0], lengths[0, 0])
-    return (
-        attention.reshape((1, 1, ny, 2, hl, lat)),
-        mix.reshape((1, 1, ny, 2, width)),
-    )
+    return pl.pallas_call(
+        placed_kernel,
+        out_shape=(
+            jax.ShapeDtypeStruct((1, 1, ny, 2, hl, lat), bf16),
+            jax.ShapeDtypeStruct((1, 1, ny, 2, width), bf16),
+        ),
+        in_specs=[vmem] * 2,
+        out_specs=(vmem, vmem),
+    )(attention, mix)
 
 
 def solution(mesh):

time: 47.1 us -> 44 us (0.934)
  local copies, waits for them, and re-layouts: 2.8 us -> 0 us
    reshape x2 -> x0, local copies, waits for them, and re-layouts: 2.8 us -> none  [the longest x1 1.47 us: shards(): mix.reshape((1, 1, ny, 2, width))]
    pallas_call x1, Pallas kernels: 43.5 us -> 41.6 us  [shards(): pl.pallas_call(functools.partial(kernel, (nd, ny, nz, nx)), out_shape=(ja...]
    pallas_call x0 -> x1, Pallas kernels: none -> 1.48 us  [shards(): pl.pallas_call(placed_kernel, out_shape=(jax.ShapeDtypeStruct((1, 1, ny,...]
where the time goes in v4:
time: 44 us; the launch traced here: 43.8 us
  Pallas kernels  43.1 us (98%)
  between operations  0.64 us (1%)
    pallas_call x1, Pallas kernels, shards(): pl.pallas_call(functools.partial(kernel, (nd, ny, nz, nx)), out_shape=(ja...  41.6 us
    pallas_call x1, Pallas kernels, shards(): pl.pallas_call(placed_kernel, out_shape=(jax.ShapeDtypeStruct((1, 1, ny,...  1.48 us

profile of v4, /device:TPU:32, one launch (start us, length us, event | category | flops | bytes accessed | tf_op | source)
XLA Modules:
  0.0 43.8 jit_solution(16470171765120479124)
XLA Ops:
  0.6 41.6 %shard_map.131 = (bf16[16,512]{1,0:T(8,128)(2,1)}, bf16[8,3584]{1,0:T(8,128)(2,1)}) custom-call(bf16[2,128,512]{2,1,0:T(8,128)(2,1)} %bitcast.11, bf16[2,576,256]{2,1,0:T(8,128)(2,1)} %bitcast.10, bf16[2,3584,128]{2,1,0:T(8,128)(2,1)} %up_h.1, bf16[2,128,3584]{2,1,0:T(8,128)(2,1)} %dn_h.1, bf16[2,64,128]{2,1,0:T(8,128)(2,1)} %bitcast.12, ...), custom_call_target="tpu_custom_call" | custom-call | tf_op jit(solution)/shard_map/pallas_call | solution.py:423
  42.3 1.5 %shard_map.132 = (bf16[1,1,4,2,2,512]{5,4,3,2,1,0:T(2,128)(2,1)}, bf16[1,1,4,2,3584]{4,3,2,1,0:T(2,128)(2,1)}) custom-call(bf16[16,512]{1,0:T(8,128)(2,1)} %get-tuple-element.4.attention, bf16[8,3584]{1,0:T(8,128)(2,1)} %get-tuple-element.5.mix), custom_call_target="tpu_custom_call" | custom-call | tf_op jit(solution)/shard_map/pallas_call | solution.py:472

commit v5 on v4

--- a/solution.py
+++ b/solution.py
@@ -46,7 +46,7 @@
     cv, q, up, dn, cr, cs, nk, xr, ids, gates, owners, lengths, tr, nkp, xf, xg,
     a1s, a1r, t1s, t1r, a2s, a2r, a3s, a3r,
     e1s, e1r, e2s, e2r, e3s, e3r, e5,
-    in_sem,
+    in_sem, line_in,
     e0_ss, e0_rs, a1_ss, a1_rs, t1_ss, t1_rs, a2_ss, a2_rs, a3_ss, a3_rs,
     e1_ss, e1_rs, e2_ss, e2_rs, e3_ss, e3_rs, e5_ss, e5_rs,
 ):
@@ -163,11 +163,12 @@
 
         return act
 
-    each(1, nd, greet(plane))
-    each(1, pairs, greet(far))
-    for k in range(1, spots):
-        if k % corners:
-            greet(both_planes)(k)
+    for k in far_order:
+        greet(far)(k)
+    for k in near_order:
+        greet(near)(k)
+    for k in plane_order:
+        greet(plane)(k)
 
     loads = {}
     for n, (name, src, dst) in enumerate((
@@ -201,16 +202,24 @@
         nkp[16 * r:16 * r + 2, :] = nk[r].astype(f32)
     scale_cols = tr[:, :ctx].T
     total_rows = corners * rows_x
-    place = iota((total_rows, cols), 0)
     per = 2 * hl
-    h_of = lax.rem(place, hl)
-    j_of = lax.rem(place // hl, 2)
-    r_of = lax.rem(place // per, 2)
-    pair_of = lax.rem(place // (2 * per), pairs)
-    side_of = lax.rem(place // (2 * per * pairs), 2)
-    x_of = place // (4 * per * pairs)
-    z_of = pair_of * 2 + side_of
-    match = (j_of * heads + (z_of * nx + x_of) * hl + h_of) == iota((total_rows, cols), 1)
+    place = iota((total_rows, heads), 0)
+    shift = lambda n: n.bit_length() - 1
+    h_of = place & (hl - 1)
+    j_of = (place >> shift(hl)) & 1
+    r_of = (place >> shift(per)) & 1
+    pair_of = (place >> shift(2 * per)) & (pairs - 1)
+    side_of = (place >> shift(2 * per * pairs)) & 1
+    x_of = place >> shift(4 * per * pairs)
+    head_of = ((pair_of * 2 + side_of) * nx + x_of) * hl + h_of
+    match = head_of == iota((total_rows, heads), 1)
+    orders = [
+        jnp.concatenate(
+            [jnp.where(match & (r_of == r) & (j_of == j), 1.0, 0.0).astype(bf16) for j in range(2)],
+            axis=1,
+        )
+        for r in range(2)
+    ]
     for name in ("values", "queries", "rope", "lengths"):
         loads[name].wait()
     out = jnp.zeros((total_rows, lat), f32)
@@ -240,7 +249,7 @@
         extra = jnp.zeros((16, cols), f32)
         for n, part in enumerate(three_parts(peak) + three_parts(total)):
             extra = jnp.where(line == n, part, extra)
-        order = jnp.where(match & (r_of == r), 1.0, 0.0).astype(bf16)
+        order = orders[r]
         out = out + dot(dot_rows(order, cached.astype(bf16)).astype(bf16), latent)
         out = out + dot(dot_rows(order, newer.astype(bf16)).astype(bf16), fresh[:, :lat])
         stats = stats + dot_rows(extra.astype(bf16), order)
@@ -251,8 +260,10 @@
         a1s[to] = out[to * rows_x:(to + 1) * rows_x].astype(bf16)
         t1s[to, 0:1, :rows_x] = peak[:, to * rows_x:(to + 1) * rows_x]
         t1s[to, 1:2, :rows_x] = total[:, to * rows_x:(to + 1) * rows_x]
-    pl.semaphore_wait(barrier, (pairs - 1) + (nd - 1) + (spots - ny))
+    pl.semaphore_wait(barrier, (pairs - 1) + (nd - 1) + (corners - 1))
     start(c_e0, plane_order)
+    for k in near_order:
+        pl.semaphore_signal(line_in, inc=1, device_id=near(k)[1], device_id_type=MESH)
     start(c_t1, near_order)
     start(c_a1, near_order)
 
@@ -300,6 +311,7 @@
         c_e1(j).start()
         owns[j] = jnp.where(s == 0, second, first)
 
+    pl.semaphore_wait(line_in, corners - 1)
     for j in strips:
         c_e1(j).wait_recv()
         own = owns[j] + e1r[j].astype(f32)
@@ -460,7 +472,7 @@
             pltpu.VMEM((sec, block), bf16),
             pltpu.VMEM((pairs, sec, block), bf16),
             pltpu.VMEM((spots, sec, block), bf16),
-            sems(12),
+            sems(12), pltpu.SemaphoreType.REGULAR,
             sems(nd), sems(nd), sems(corners), sems(corners), sems(corners), sems(corners),
             sems(pairs), sems(pairs), sems(ny), sems(ny),
             sems(ny), sems(ny), sems(spots), sems(spots), sems(pairs), sems(pairs), sems(spots), sems(spots),

time: 44 us -> 43.8 us (level)
  the two profiles are of different devices: /device:TPU:32 before, /device:TPU:2 now
where the time goes in v5:
time: 43.8 us; the launch traced here: 43.6 us
  Pallas kernels  43 us (98%)
  between operations  0.64 us (1%)
    pallas_call x1, Pallas kernels, shards(): pl.pallas_call(functools.partial(kernel, (nd, ny, nz, nx)), out_shape=(ja...  41.5 us
    pallas_call x1, Pallas kernels, shards(): pl.pallas_call(placed_kernel, out_shape=(jax.ShapeDtypeStruct((1, 1, ny,...  1.48 us

profile of v5, /device:TPU:2, one launch (start us, length us, event | category | flops | bytes accessed | tf_op | source)
XLA Modules:
  0.0 43.6 jit_solution(8612236365216952778)
XLA Ops:
  0.6 41.5 %shard_map.131 = (bf16[16,512]{1,0:T(8,128)(2,1)}, bf16[8,3584]{1,0:T(8,128)(2,1)}) custom-call(bf16[2,128,512]{2,1,0:T(8,128)(2,1)} %bitcast.11, bf16[2,576,256]{2,1,0:T(8,128)(2,1)} %bitcast.10, bf16[2,3584,128]{2,1,0:T(8,128)(2,1)} %up_h.1, bf16[2,128,3584]{2,1,0:T(8,128)(2,1)} %dn_h.1, bf16[2,64,128]{2,1,0:T(8,128)(2,1)} %bitcast.12, ...), custom_call_target="tpu_custom_call" | custom-call | tf_op jit(solution)/shard_map/pallas_call | solution.py:435
  42.1 1.5 %shard_map.132 = (bf16[1,1,4,2,2,512]{5,4,3,2,1,0:T(2,128)(2,1)}, bf16[1,1,4,2,3584]{4,3,2,1,0:T(2,128)(2,1)}) custom-call(bf16[16,512]{1,0:T(8,128)(2,1)} %get-tuple-element.4.attention, bf16[8,3584]{1,0:T(8,128)(2,1)} %get-tuple-element.5.mix), custom_call_target="tpu_custom_call" | custom-call | tf_op jit(solution)/shard_map/pallas_call | solution.py:484
